TPU v7x, 1024 devices: a whole 8x8x8 slice. The times are simulated.
1024 devices in a mesh: gx: 64 (over y, z), gy: 16 (over x, core).
Axes of the slice: x: 8, y: 8, z: 8, core: 2. Of those that a mesh axis runs over, the one named last changes fastest.
Arguments:
- features: bfloat16 [8, 64, 512, 2048], P(None, None, 'gx', 'gy'), may hold values from -6 to 6
- head_weight: bfloat16 [6, 64], replicated, may hold values from -0.75 to 0.75
- head_bias: float32 [6], replicated, may hold values from -1 to 1
- probs: float32 [8, 8, 512, 2048], P(None, None, 'gx', 'gy'), may hold values from 0 to 1
- cotangent: float32 [8, 8, 512, 2048], P(None, None, 'gx', 'gy'), may hold values from -12 to 12
Outputs:
- grad_probs: float32 [8, 8, 512, 2048], P(None, None, 'gx', 'gy')
- grad_weight: float32 [6, 64], replicated
- grad_bias: float32 [6], replicated
All inputs are finite; a program needn't handle non-finite values.
Results may differ from a plain program's by a relative error of at most 0.0027.
Values sent between devices are 32-bit elements; how exact they have to be, the bound alone decides.
A program may use at most 32 MiB of HBM per device.

v0:
```python
import math

import jax
import jax.numpy as jnp
from jax import lax
from jax.sharding import PartitionSpec as P

ITERS = 3


def with_halo(cells, sides, width):
    for axis, dim in sides:
        count = lax.axis_size(axis)
        ends = count - 1
        head = lax.slice_in_dim(cells, 0, width, axis=dim)
        tail = lax.slice_in_dim(cells, cells.shape[dim] - width, cells.shape[dim], axis=dim)
        cells = jnp.concatenate(
            [
                lax.ppermute(tail, axis, [(i, (i + 1) % count) for i in range(ends)]),
                cells,
                lax.ppermute(head, axis, [((i + 1) % count, i) for i in range(ends)]),
            ],
            axis=dim,
        )
    return cells


def along_depth(field, offset):
    blank = jnp.zeros_like(field[:1])
    if offset > 0:
        return jnp.concatenate([field[1:], blank], 0)
    return jnp.concatenate([blank, field[:-1]], 0)


def neighbours(padded):
    middle = padded[:, :, 1:-1, 1:-1]
    beside = [
        padded[:, :, 2:, 1:-1],
        padded[:, :, :-2, 1:-1],
        padded[:, :, 1:-1, 2:],
        padded[:, :, 1:-1, :-2],
        along_depth(middle, 1),
        along_depth(middle, -1),
    ]
    return (beside, middle)


def propagate(padded, coupling):
    beside, middle = neighbours(padded)
    centre = 1.0 - jnp.sum(coupling, 0)
    result = centre[:, None] * middle
    for direction in range(6):
        result = result + coupling[direction][:, None] * beside[direction]
    return result


def transpose_step(padded, coupling):
    centre = (1.0 - jnp.sum(coupling, 0))[:, 1:-1, 1:-1]
    pushed = [coupling[direction][:, None] * padded for direction in range(6)]
    middle = padded[:, :, 1:-1, 1:-1]
    result = centre[:, None] * middle
    result = result + pushed[0][:, :, :-2, 1:-1] + pushed[1][:, :, 2:, 1:-1]
    result = result + pushed[2][:, :, 1:-1, :-2] + pushed[3][:, :, 1:-1, 2:]
    result = (
        result
        + along_depth(pushed[4][:, :, 1:-1, 1:-1], -1)
        + along_depth(pushed[5][:, :, 1:-1, 1:-1], 1)
    )
    return result


def local_terms(grad_field, prob_pad):
    beside, middle = neighbours(prob_pad)
    kappa_grad = jnp.stack(
        [jnp.sum(grad_field * beside[direction], 1) for direction in range(6)], 0
    )
    centre_grad = jnp.sum(grad_field * middle, 1)
    return (kappa_grad, centre_grad)


def rim_probs(field, width):
    return with_halo(field, (("gx", 2), ("gy", 3)), width)


def rim_cot(field, width):
    return with_halo(field, (("gx", 2), ("gy", 3)), width)


def rim_coupling(coupling, width):
    return with_halo(coupling, (("gx", 2), ("gy", 3)), width)


def per_device(features, head_weight, head_bias, probs, cotangent):
    logits = (
        jnp.einsum("kf,zfxy->kzxy", head_weight, features, preferred_element_type=jnp.float32)
        + head_bias[:, None, None, None]
    )
    active = jax.nn.sigmoid(logits)
    summed = jnp.sum(active, 0)
    coupling = active / (summed + 1.0)
    kappa_grad = jnp.zeros_like(coupling)
    centre_grad = jnp.zeros_like(summed)
    coupling_pad = rim_coupling(coupling, 1)
    history = []
    current = probs
    for iteration in range(ITERS):
        prob_pad = rim_probs(current, 1)
        history.append(prob_pad)
        if iteration + 1 < ITERS:
            current = propagate(prob_pad, coupling)
    grad_field = cotangent
    for iteration in reversed(range(ITERS)):
        cot_pad = rim_cot(grad_field, 1)
        kappa_part, centre_part = local_terms(grad_field, history[iteration])
        kappa_grad = kappa_grad + kappa_part
        centre_grad = centre_grad + centre_part
        grad_field = transpose_step(cot_pad, coupling_pad)
    effective = kappa_grad - centre_grad[None]
    active_grad = (effective - jnp.sum(effective * coupling, 0)[None]) / (summed + 1.0)[None]
    logit_grad = active_grad * active * (1.0 - active)
    weight_part = jnp.einsum(
        "kzxy,zfxy->kf",
        logit_grad.astype(jnp.bfloat16),
        features,
        preferred_element_type=jnp.float32,
    )
    bias_part = jnp.sum(logit_grad, (1, 2, 3))
    weight_sum, bias_sum = lax.psum((weight_part, bias_part), ("gx", "gy"))
    voxel_count = (
        features.shape[0]
        * features.shape[2]
        * features.shape[3]
        * lax.axis_size("gx")
        * lax.axis_size("gy")
    )
    factor = 1.0 / math.sqrt(voxel_count)
    return (grad_field, weight_sum * factor, bias_sum * factor)


def solution(mesh):
    in_specs = (
        P(None, None, "gx", "gy"),
        P(),
        P(),
        P(None, None, "gx", "gy"),
        P(None, None, "gx", "gy"),
    )
    out_specs = (P(None, None, "gx", "gy"), P(), P())
    return jax.shard_map(
        per_device, mesh=mesh, in_specs=in_specs, out_specs=out_specs, check_vma=False
    )
```

profile of v0, /device:TPU:1, one launch (start us, length us, event | category | flops | bytes accessed | tf_op | source)
XLA Modules:
  0.0 277.3 jit_solution(600579908367532994)
XLA Ops:
  0.6 1.2 copy-done
  1.9 1.0 fusion.46
  2.9 0.7 copy-done.23
  3.7 5.9 %collective-permute-start = (f32[6,8,1,128]{3,0,2,1:T(8,128)S(1)}, f32[6,8,1,128]{3,0,2,1:T(8,128)S(1)}, u32[]{:S(2)}, u32[]{:S(2)}) collective-permute-start(f32[6,8,1,128]{3,0,2,1:T(8,128)S(1)} %get-tuple-element.83), channel_id=1, source_target_pairs={{0,16},{16,32},{32,48},{48,64},{64,80},{80,96},{96,112},{112,128},... | collective-permute-start | bytes 73736 | tf_op jit(solution)/shard_map/ppermute | solution.py:19
  9.6 1.3 collective-permute-start.1
  10.9 5.5 %collective-permute-start.4 = (f32[8,8,1,128]{3,2,1,0:T(1,128)S(1)}, f32[8,8,1,128]{3,2,1,0:T(1,128)S(1)}, u32[]{:S(2)}, u32[]{:S(2)}) collective-permute-start(f32[8,8,1,128]{3,2,1,0:T(1,128)S(1)} %get-tuple-element.85), channel_id=1, source_target_pairs={{0,16},{16,32},{32,48},{48,64},{64,80},{80,96},{96,112},{112,128},... | collective-permute-start | bytes 98312 | tf_op jit(solution)/shard_map/ppermute | solution.py:19
  16.5 1.3 collective-permute-start.5
  17.8 1.3 collective-permute-start.16
  19.6 4.2 %collective-permute-start.2 = (f32[6,8,10,1]{3,0,2,1:T(8,128)S(1)}, f32[6,8,10,1]{3,0,2,1:T(8,128)S(1)}, u32[]{:S(2)}, u32[]{:S(2)}) collective-permute-start(f32[6,8,10,1]{3,0,2,1:T(8,128)S(1)} %get-tuple-element.69), channel_id=1, source_target_pairs={{0,1},{1,2},{2,3},{3,4},{4,5},{5,6},{6,7},{7,8},{8,9},{9,10},{10,1... | collective-permute-start | bytes 5768 | tf_op jit(solution)/shard_map/ppermute | solution.py:19
  23.8 7.7 %collective-permute-start.3 = (f32[6,8,10,1]{3,0,2,1:T(8,128)S(1)}, f32[6,8,10,1]{3,0,2,1:T(8,128)S(1)}, u32[]{:S(2)}, u32[]{:S(2)}) collective-permute-start(f32[6,8,10,1]{3,0,2,1:T(8,128)S(1)} %get-tuple-element.70), channel_id=1, source_target_pairs={{1,0},{2,1},{3,2},{4,3},{5,4},{6,5},{7,6},{8,7},{9,8},{10,9},{11,1... | collective-permute-start | bytes 5768 | tf_op jit(solution)/shard_map/ppermute | solution.py:21
  31.5 4.9 %collective-permute-start.17 = (f32[8,8,1,128]{3,2,1,0:T(1,128)S(1)}, f32[8,8,1,128]{3,2,1,0:T(1,128)S(1)}, u32[]{:S(2)}, u32[]{:S(2)}) collective-permute-start(f32[8,8,1,128]{3,2,1,0:T(1,128)S(1)} %get-tuple-element.97), channel_id=1, source_target_pairs={{0,16},{16,32},{32,48},{48,64},{64,80},{80,96},{96,112},{112,128},... | collective-permute-start | bytes 98312 | tf_op jit(solution)/shard_map/ppermute | solution.py:19
  36.4 0.4 fusion.51
  36.8 0.3 fusion.52
  38.1 1.9 collective-permute-start.18
  40.0 3.6 %collective-permute-start.19 = (f32[8,8,10,1]{3,2,1,0:T(8,128)S(1)}, f32[8,8,10,1]{3,2,1,0:T(8,128)S(1)}, u32[]{:S(2)}, u32[]{:S(2)}) collective-permute-start(f32[8,8,10,1]{3,2,1,0:T(8,128)S(1)} %get-tuple-element.67), channel_id=1, source_target_pairs={{0,1},{1,2},{2,3},{3,4},{4,5},{5,6},{6,7},{7,8},{8,9},{9,10},{10,1... | collective-permute-start | bytes 7688 | tf_op jit(solution)/shard_map/ppermute | solution.py:19
  44.0 1.9 collective-permute-start.6
  45.9 2.4 collective-permute-start.7
  48.6 1.2 collective-permute-done.19
  49.8 0.5 fusion.11
  50.4 1.3 collective-permute-start.20
  51.7 5.5 %collective-permute-start.21 = (f32[8,8,1,128]{3,2,1,0:T(1,128)S(1)}, f32[8,8,1,128]{3,2,1,0:T(1,128)S(1)}, u32[]{:S(2)}, u32[]{:S(2)}) collective-permute-start(f32[8,8,1,128]{3,2,1,0:T(1,128)S(1)} %get-tuple-element.87), channel_id=1, source_target_pairs={{0,16},{16,32},{32,48},{48,64},{64,80},{80,96},{96,112},{112,128},... | collective-permute-start | bytes 98312 | tf_op jit(solution)/shard_map/ppermute | solution.py:19
  57.2 0.8 pad_maximum_fusion
  58.5 1.9 collective-permute-start.22
  60.4 5.2 %collective-permute-start.23 = (f32[8,8,10,1]{3,2,1,0:T(8,128)S(1)}, f32[8,8,10,1]{3,2,1,0:T(8,128)S(1)}, u32[]{:S(2)}, u32[]{:S(2)}) collective-permute-start(f32[8,8,10,1]{3,2,1,0:T(8,128)S(1)} %get-tuple-element.65), channel_id=1, source_target_pairs={{0,1},{1,2},{2,3},{3,4},{4,5},{5,6},{6,7},{7,8},{8,9},{9,10},{10,1... | collective-permute-start | bytes 7688 | tf_op jit(solution)/shard_map/ppermute | solution.py:19
  65.7 4.9 %collective-permute-done.22 = f32[8,8,10,1]{3,2,1,0:T(8,128)S(1)} collective-permute-done((f32[8,8,10,1]{3,2,1,0:T(8,128)S(1)}, f32[8,8,10,1]{3,2,1,0:T(8,128)S(1)}, u32[]{:S(2)}, u32[]{:S(2)}) %collective-permute-start.22) | collective-permute-done | bytes 2592 | tf_op jit(solution)/shard_map/ppermute | solution.py:21
  70.6 1.2 collective-permute-done.23
  71.8 0.5 fusion.15
  72.3 0.8 fusion.62
  73.1 1.4 fusion.17
  74.5 0.7 fusion.64
  75.2 5.5 %collective-permute-start.8 = (f32[8,8,1,128]{3,2,1,0:T(1,128)}, f32[8,8,1,128]{3,2,1,0:T(1,128)}, u32[]{:S(2)}, u32[]{:S(2)}) collective-permute-start(f32[8,8,1,128]{3,2,1,0:T(1,128)} %get-tuple-element.81), channel_id=1, source_target_pairs={{0,16},{16,32},{32,48},{48,64},{64,80},{80,96},{96,112},{112,128},... | collective-permute-start | bytes 98312 | tf_op jit(solution)/shard_map/ppermute | solution.py:19
  80.7 1.3 collective-permute-start.9
  82.0 0.7 fusion.61
  82.7 1.3 collective-permute-start.24
  84.0 5.5 %collective-permute-start.25 = (f32[8,8,1,128]{3,2,1,0:T(1,128)}, f32[8,8,1,128]{3,2,1,0:T(1,128)S(1)}, u32[]{:S(2)}, u32[]{:S(2)}) collective-permute-start(f32[8,8,1,128]{3,2,1,0:T(1,128)} %get-tuple-element.75), channel_id=1, source_target_pairs={{0,16},{16,32},{32,48},{48,64},{64,80},{80,96},{96,112},{112,128},... | collective-permute-start | bytes 98312 | tf_op jit(solution)/shard_map/ppermute | solution.py:19
  89.5 1.0 stack.76
  90.5 0.9 pad_maximum_fusion.5
  91.6 4.9 %collective-permute-start.10 = (f32[8,8,10,1]{3,2,1,0:T(8,128)S(1)}, f32[8,8,10,1]{3,2,1,0:T(8,128)S(1)}, u32[]{:S(2)}, u32[]{:S(2)}) collective-permute-start(f32[8,8,10,1]{3,2,1,0:T(8,128)S(1)} %get-tuple-element.61), channel_id=1, source_target_pairs={{0,1},{1,2},{2,3},{3,4},{4,5},{5,6},{6,7},{7,8},{8,9},{9,10},{10,1... | collective-permute-start | bytes 7688 | tf_op jit(solution)/shard_map/ppermute | solution.py:19
  96.6 1.9 collective-permute-start.11
  98.6 0.5 copy-done.38
  99.3 1.9 collective-permute-start.26
  101.3 4.0 %collective-permute-start.27 = (f32[8,8,10,1]{3,2,1,0:T(8,128)S(1)}, f32[8,8,10,1]{3,2,1,0:T(8,128)S(1)}, u32[]{:S(2)}, u32[]{:S(2)}) collective-permute-start(f32[8,8,10,1]{3,2,1,0:T(8,128)S(1)} %get-tuple-element.57), channel_id=1, source_target_pairs={{0,1},{1,2},{2,3},{3,4},{4,5},{5,6},{6,7},{7,8},{8,9},{9,10},{10,1... | collective-permute-start | bytes 7688 | tf_op jit(solution)/shard_map/ppermute | solution.py:19
  105.3 1.8 collective-permute-done.11
  107.1 1.5 pad_maximum_fusion.1
  108.9 0.7 copy-done.4
  109.7 1.4 fusion.13
  111.2 1.5 collective-permute-done.26
  112.7 0.5 multiply_reduce_fusion.11
  113.6 0.3 stack.69
  113.9 0.4 copy-done.25
  115.1 0.3 fusion.60
  115.5 0.4 convolution_bitcast_fusion
  115.9 5.2 %collective-permute-start.12 = (f32[8,8,1,128]{3,2,1,0:T(1,128)S(1)}, f32[8,8,1,128]{3,2,1,0:T(1,128)S(1)}, u32[]{:S(2)}, u32[]{:S(2)}) collective-permute-start(f32[8,8,1,128]{3,2,1,0:T(1,128)S(1)} %get-tuple-element.79), channel_id=1, source_target_pairs={{0,16},{16,32},{32,48},{48,64},{64,80},{80,96},{96,112},{112,128},... | collective-permute-start | bytes 98312 | tf_op jit(solution)/shard_map/ppermute | solution.py:19
  121.1 1.3 collective-permute-start.13
  122.4 138.9 %all-reduce.12 = (f32[6,64]{1,0:T(8,128)S(1)}, f32[6]{0:T(128)S(1)}) all-reduce(f32[6,64]{1,0:T(8,128)S(1)} %convolution_bitcast_fusion, f32[6]{0:T(128)S(1)} %get-tuple-element.73), channel_id=1, replica_groups=mesh['gx'=64,'gy'=16] {'gx','gy'}, use_global_device_ids=true, to_apply=%region_25.0 | all-reduce | flops 390 | bytes 3120 | tf_op jit(solution)/shard_map/psum | solution.py:128
  261.3 0.6 broadcast_multiply_fusion
  262.2 2.1 collective-permute-start.14
  264.3 2.3 collective-permute-start.15
  266.5 0.5 broadcast_multiply_fusion.1
  267.1 3.3 %collective-permute-done.14 = f32[8,8,10,1]{3,2,1,0:T(8,128)S(1)} collective-permute-done((f32[8,8,10,1]{3,2,1,0:T(8,128)S(1)}, f32[8,8,10,1]{3,2,1,0:T(8,128)S(1)}, u32[]{:S(2)}, u32[]{:S(2)}) %collective-permute-start.14) | collective-permute-done | bytes 2592 | tf_op jit(solution)/shard_map/ppermute | solution.py:19
  270.4 4.4 %collective-permute-done.15 = f32[8,8,10,1]{3,2,1,0:T(8,128)S(1)} collective-permute-done((f32[8,8,10,1]{3,2,1,0:T(8,128)S(1)}, f32[8,8,10,1]{3,2,1,0:T(8,128)S(1)}, u32[]{:S(2)}, u32[]{:S(2)}) %collective-permute-start.15) | collective-permute-done | bytes 2592 | tf_op jit(solution)/shard_map/ppermute | solution.py:21
  274.8 0.7 pad_maximum_fusion.2
  275.7 0.6 copy-done.11
  276.3 1.0 fusion.28
  (142 shorter events, 5.2 us)
Async XLA Ops:
  0.6 1.2 copy-start
  2.9 0.8 copy-start.42
  3.5 7.3 %copy-start.2 = (f32[8,8,8,128]{3,2,1,0:T(8,128)S(1)}, f32[8,8,8,128]{3,2,1,0:T(8,128)}, u32[]{:S(2)}) copy-start(f32[8,8,8,128]{3,2,1,0:T(8,128)} %param.9) | copy-start | bytes 786436
  3.7 14.1 %copy-start.1 = (f32[8,8,8,128]{3,2,1,0:T(8,128)S(1)}, f32[8,8,8,128]{3,2,1,0:T(8,128)}, u32[]{:S(2)}) copy-start(f32[8,8,8,128]{3,2,1,0:T(8,128)} %param.8) | copy-start | bytes 786436
  3.7 15.7 %collective-permute-start = (f32[6,8,1,128]{3,0,2,1:T(8,128)S(1)}, f32[6,8,1,128]{3,0,2,1:T(8,128)S(1)}, u32[]{:S(2)}, u32[]{:S(2)}) collective-permute-start(f32[6,8,1,128]{3,0,2,1:T(8,128)S(1)} %get-tuple-element.83), channel_id=1, source_target_pairs={{0,16},{16,32},{32,48},{48,64},{64,80},{80,96},{96,112},{112,128},... | collective-permute-start | bytes 73736 | tf_op jit(solution)/shard_map/ppermute | solution.py:19
  9.6 9.8 %collective-permute-start.1 = (f32[6,8,1,128]{3,0,2,1:T(8,128)S(1)}, f32[6,8,1,128]{3,0,2,1:T(8,128)S(1)}, u32[]{:S(2)}, u32[]{:S(2)}) collective-permute-start(f32[6,8,1,128]{3,0,2,1:T(8,128)S(1)} %get-tuple-element.84), channel_id=1, source_target_pairs={{16,0},{32,16},{48,32},{64,48},{80,64},{96,80},{112,96},{128,112},... | collective-permute-start | bytes 73736 | tf_op jit(solution)/shard_map/ppermute | solution.py:21
  10.9 32.8 %collective-permute-start.4 = (f32[8,8,1,128]{3,2,1,0:T(1,128)S(1)}, f32[8,8,1,128]{3,2,1,0:T(1,128)S(1)}, u32[]{:S(2)}, u32[]{:S(2)}) collective-permute-start(f32[8,8,1,128]{3,2,1,0:T(1,128)S(1)} %get-tuple-element.85), channel_id=1, source_target_pairs={{0,16},{16,32},{32,48},{48,64},{64,80},{80,96},{96,112},{112,128},... | collective-permute-start | bytes 98312 | tf_op jit(solution)/shard_map/ppermute | solution.py:19
  16.5 27.2 %collective-permute-start.5 = (f32[8,8,1,128]{3,2,1,0:T(1,128)S(1)}, f32[8,8,1,128]{3,2,1,0:T(1,128)S(1)}, u32[]{:S(2)}, u32[]{:S(2)}) collective-permute-start(f32[8,8,1,128]{3,2,1,0:T(1,128)S(1)} %get-tuple-element.86), channel_id=1, source_target_pairs={{16,0},{32,16},{48,32},{64,48},{80,64},{96,80},{112,96},{128,112},... | collective-permute-start | bytes 98312 | tf_op jit(solution)/shard_map/ppermute | solution.py:21
  17.8 19.9 %collective-permute-start.16 = (f32[8,8,1,128]{3,2,1,0:T(1,128)S(1)}, f32[8,8,1,128]{3,2,1,0:T(1,128)S(1)}, u32[]{:S(2)}, u32[]{:S(2)}) collective-permute-start(f32[8,8,1,128]{3,2,1,0:T(1,128)S(1)} %get-tuple-element.98), channel_id=1, source_target_pairs={{16,0},{32,16},{48,32},{64,48},{80,64},{96,80},{112,96},{128,112},... | collective-permute-start | bytes 98312 | tf_op jit(solution)/shard_map/ppermute | solution.py:21
  19.2 30.6 %copy-start.3 = (f32[7,8,8,128]{3,2,1,0:T(8,128)}, f32[7,8,8,128]{3,2,1,0:T(8,128)S(1)}, u32[]{:S(2)}) copy-start(f32[7,8,8,128]{3,2,1,0:T(8,128)S(1)} %get-tuple-element.99) | copy-start | bytes 688132
  19.2 30.6 %copy-start.5 = (f32[7,8,8,128]{3,2,1,0:T(8,128)}, f32[7,8,8,128]{3,2,1,0:T(8,128)S(1)}, u32[]{:S(2)}) copy-start(f32[7,8,8,128]{3,2,1,0:T(8,128)S(1)} %get-tuple-element.100) | copy-start | bytes 688132
  19.6 12.0 %collective-permute-start.2 = (f32[6,8,10,1]{3,0,2,1:T(8,128)S(1)}, f32[6,8,10,1]{3,0,2,1:T(8,128)S(1)}, u32[]{:S(2)}, u32[]{:S(2)}) collective-permute-start(f32[6,8,10,1]{3,0,2,1:T(8,128)S(1)} %get-tuple-element.69), channel_id=1, source_target_pairs={{0,1},{1,2},{2,3},{3,4},{4,5},{5,6},{6,7},{7,8},{8,9},{9,10},{10,1... | collective-permute-start | bytes 5768 | tf_op jit(solution)/shard_map/ppermute | solution.py:19
  23.8 12.6 %collective-permute-start.3 = (f32[6,8,10,1]{3,0,2,1:T(8,128)S(1)}, f32[6,8,10,1]{3,0,2,1:T(8,128)S(1)}, u32[]{:S(2)}, u32[]{:S(2)}) collective-permute-start(f32[6,8,10,1]{3,0,2,1:T(8,128)S(1)} %get-tuple-element.70), channel_id=1, source_target_pairs={{1,0},{2,1},{3,2},{4,3},{5,4},{6,5},{7,6},{8,7},{9,8},{10,9},{11,1... | collective-permute-start | bytes 5768 | tf_op jit(solution)/shard_map/ppermute | solution.py:21
  31.5 6.2 %collective-permute-start.17 = (f32[8,8,1,128]{3,2,1,0:T(1,128)S(1)}, f32[8,8,1,128]{3,2,1,0:T(1,128)S(1)}, u32[]{:S(2)}, u32[]{:S(2)}) collective-permute-start(f32[8,8,1,128]{3,2,1,0:T(1,128)S(1)} %get-tuple-element.97), channel_id=1, source_target_pairs={{0,16},{16,32},{32,48},{48,64},{64,80},{80,96},{96,112},{112,128},... | collective-permute-start | bytes 98312 | tf_op jit(solution)/shard_map/ppermute | solution.py:19
  37.4 20.6 %copy-start.12 = (f32[7,8,128]{2,1,0:T(8,128)}, f32[7,8,128]{2,1,0:T(8,128)S(1)}, u32[]{:S(2)}) copy-start(f32[7,8,128]{2,1,0:T(8,128)S(1)} %slice.384) | copy-start | bytes 86020
  37.5 20.5 %copy-start.15 = (f32[7,8,128]{2,1,0:T(8,128)}, f32[7,8,128]{2,1,0:T(8,128)S(1)}, u32[]{:S(2)}) copy-start(f32[7,8,128]{2,1,0:T(8,128)S(1)} %slice.387) | copy-start | bytes 86020
  37.8 35.4 %copy-start.9 = (f32[8,8,128]{2,1,0:T(8,128)}, f32[8,8,128]{2,1,0:T(8,128)S(1)}, u32[]{:S(2)}) copy-start(f32[8,8,128]{2,1,0:T(8,128)S(1)} %slice.381) | copy-start | bytes 98308
  37.8 12.0 %copy-start.18 = (f32[8,8,1,128]{3,2,1,0:T(1,128)}, f32[8,8,1,128]{3,2,1,0:T(1,128)S(1)}, u32[]{:S(2)}) copy-start(f32[8,8,1,128]{3,2,1,0:T(1,128)S(1)} %collective-permute-done.16) | copy-start | bytes 98308
  37.8 12.0 %copy-start.20 = (f32[8,8,1,128]{3,2,1,0:T(1,128)}, f32[8,8,1,128]{3,2,1,0:T(1,128)S(1)}, u32[]{:S(2)}) copy-start(f32[8,8,1,128]{3,2,1,0:T(1,128)S(1)} %collective-permute-done.17) | copy-start | bytes 98308
  38.1 10.5 %collective-permute-start.18 = (f32[8,8,10,1]{3,2,1,0:T(8,128)S(1)}, f32[8,8,10,1]{3,2,1,0:T(8,128)S(1)}, u32[]{:S(2)}, u32[]{:S(2)}) collective-permute-start(f32[8,8,10,1]{3,2,1,0:T(8,128)S(1)} %get-tuple-element.68), channel_id=1, source_target_pairs={{1,0},{2,1},{3,2},{4,3},{5,4},{6,5},{7,6},{8,7},{9,8},{10,9},{11,1... | collective-permute-start | bytes 7688 | tf_op jit(solution)/shard_map/ppermute | solution.py:21
  40.0 9.8 %collective-permute-start.19 = (f32[8,8,10,1]{3,2,1,0:T(8,128)S(1)}, f32[8,8,10,1]{3,2,1,0:T(8,128)S(1)}, u32[]{:S(2)}, u32[]{:S(2)}) collective-permute-start(f32[8,8,10,1]{3,2,1,0:T(8,128)S(1)} %get-tuple-element.67), channel_id=1, source_target_pairs={{0,1},{1,2},{2,3},{3,4},{4,5},{5,6},{6,7},{7,8},{8,9},{9,10},{10,1... | collective-permute-start | bytes 7688 | tf_op jit(solution)/shard_map/ppermute | solution.py:19
  44.0 13.2 %collective-permute-start.6 = (f32[8,8,10,1]{3,2,1,0:T(8,128)S(1)}, f32[8,8,10,1]{3,2,1,0:T(8,128)S(1)}, u32[]{:S(2)}, u32[]{:S(2)}) collective-permute-start(f32[8,8,10,1]{3,2,1,0:T(8,128)S(1)} %get-tuple-element.63), channel_id=1, source_target_pairs={{0,1},{1,2},{2,3},{3,4},{4,5},{5,6},{6,7},{7,8},{8,9},{9,10},{10,1... | collective-permute-start | bytes 7688 | tf_op jit(solution)/shard_map/ppermute | solution.py:19
  45.9 11.3 %collective-permute-start.7 = (f32[8,8,10,1]{3,2,1,0:T(8,128)S(1)}, f32[8,8,10,1]{3,2,1,0:T(8,128)S(1)}, u32[]{:S(2)}, u32[]{:S(2)}) collective-permute-start(f32[8,8,10,1]{3,2,1,0:T(8,128)S(1)} %get-tuple-element.64), channel_id=1, source_target_pairs={{1,0},{2,1},{3,2},{4,3},{5,4},{6,5},{7,6},{8,7},{9,8},{10,9},{11,1... | collective-permute-start | bytes 7688 | tf_op jit(solution)/shard_map/ppermute | solution.py:21
  50.4 7.8 %collective-permute-start.20 = (f32[8,8,1,128]{3,2,1,0:T(1,128)S(1)}, f32[8,8,1,128]{3,2,1,0:T(1,128)S(1)}, u32[]{:S(2)}, u32[]{:S(2)}) collective-permute-start(f32[8,8,1,128]{3,2,1,0:T(1,128)S(1)} %get-tuple-element.88), channel_id=1, source_target_pairs={{16,0},{32,16},{48,32},{64,48},{80,64},{96,80},{112,96},{128,112},... | collective-permute-start | bytes 98312 | tf_op jit(solution)/shard_map/ppermute | solution.py:21
  51.7 6.5 %collective-permute-start.21 = (f32[8,8,1,128]{3,2,1,0:T(1,128)S(1)}, f32[8,8,1,128]{3,2,1,0:T(1,128)S(1)}, u32[]{:S(2)}, u32[]{:S(2)}) collective-permute-start(f32[8,8,1,128]{3,2,1,0:T(1,128)S(1)} %get-tuple-element.87), channel_id=1, source_target_pairs={{0,16},{16,32},{32,48},{48,64},{64,80},{80,96},{96,112},{112,128},... | collective-permute-start | bytes 98312 | tf_op jit(solution)/shard_map/ppermute | solution.py:19
  58.5 12.1 %collective-permute-start.22 = (f32[8,8,10,1]{3,2,1,0:T(8,128)S(1)}, f32[8,8,10,1]{3,2,1,0:T(8,128)S(1)}, u32[]{:S(2)}, u32[]{:S(2)}) collective-permute-start(f32[8,8,10,1]{3,2,1,0:T(8,128)S(1)} %get-tuple-element.66), channel_id=1, source_target_pairs={{1,0},{2,1},{3,2},{4,3},{5,4},{6,5},{7,6},{8,7},{9,8},{10,9},{11,1... | collective-permute-start | bytes 7688 | tf_op jit(solution)/shard_map/ppermute | solution.py:21
  60.4 11.3 %collective-permute-start.23 = (f32[8,8,10,1]{3,2,1,0:T(8,128)S(1)}, f32[8,8,10,1]{3,2,1,0:T(8,128)S(1)}, u32[]{:S(2)}, u32[]{:S(2)}) collective-permute-start(f32[8,8,10,1]{3,2,1,0:T(8,128)S(1)} %get-tuple-element.65), channel_id=1, source_target_pairs={{0,1},{1,2},{2,3},{3,4},{4,5},{5,6},{6,7},{7,8},{8,9},{9,10},{10,1... | collective-permute-start | bytes 7688 | tf_op jit(solution)/shard_map/ppermute | solution.py:19
  74.5 14.9 %copy-start.35 = (f32[8,8,128]{2,1,0:T(8,128)S(1)}, f32[8,8,128]{2,1,0:T(8,128)}, u32[]{:S(2)}) copy-start(f32[8,8,128]{2,1,0:T(8,128)} %get-tuple-element.23) | copy-start | bytes 98308
  74.5 14.9 %copy-start.36 = (f32[8,8,128]{2,1,0:T(8,128)S(1)}, f32[8,8,128]{2,1,0:T(8,128)}, u32[]{:S(2)}) copy-start(f32[8,8,128]{2,1,0:T(8,128)} %get-tuple-element.24) | copy-start | bytes 98308
  75.2 15.3 %collective-permute-start.8 = (f32[8,8,1,128]{3,2,1,0:T(1,128)}, f32[8,8,1,128]{3,2,1,0:T(1,128)}, u32[]{:S(2)}, u32[]{:S(2)}) collective-permute-start(f32[8,8,1,128]{3,2,1,0:T(1,128)} %get-tuple-element.81), channel_id=1, source_target_pairs={{0,16},{16,32},{32,48},{48,64},{64,80},{80,96},{96,112},{112,128},... | collective-permute-start | bytes 98312 | tf_op jit(solution)/shard_map/ppermute | solution.py:19
  80.7 9.9 %collective-permute-start.9 = (f32[8,8,1,128]{3,2,1,0:T(1,128)}, f32[8,8,1,128]{3,2,1,0:T(1,128)}, u32[]{:S(2)}, u32[]{:S(2)}) collective-permute-start(f32[8,8,1,128]{3,2,1,0:T(1,128)} %get-tuple-element.82), channel_id=1, source_target_pairs={{16,0},{32,16},{48,32},{64,48},{80,64},{96,80},{112,96},{128,112},... | collective-permute-start | bytes 98312 | tf_op jit(solution)/shard_map/ppermute | solution.py:21
  82.0 7.5 %copy-start.31 = (f32[8,8,128]{2,1,0:T(8,128)S(1)}, f32[8,8,128]{2,1,0:T(8,128)}, u32[]{:S(2)}) copy-start(f32[8,8,128]{2,1,0:T(8,128)} %get-tuple-element.18) | copy-start | bytes 98308
  82.0 7.5 %copy-start.32 = (f32[8,8,128]{2,1,0:T(8,128)S(1)}, f32[8,8,128]{2,1,0:T(8,128)}, u32[]{:S(2)}) copy-start(f32[8,8,128]{2,1,0:T(8,128)} %get-tuple-element.19) | copy-start | bytes 98308
  82.0 7.5 %copy-start.33 = (f32[8,8,128]{2,1,0:T(8,128)S(1)}, f32[8,8,128]{2,1,0:T(8,128)}, u32[]{:S(2)}) copy-start(f32[8,8,128]{2,1,0:T(8,128)} %get-tuple-element.21) | copy-start | bytes 98308
  82.0 7.5 %copy-start.34 = (f32[8,8,128]{2,1,0:T(8,128)S(1)}, f32[8,8,128]{2,1,0:T(8,128)}, u32[]{:S(2)}) copy-start(f32[8,8,128]{2,1,0:T(8,128)} %get-tuple-element.22) | copy-start | bytes 98308
  82.7 15.8 %collective-permute-start.24 = (f32[8,8,1,128]{3,2,1,0:T(1,128)}, f32[8,8,1,128]{3,2,1,0:T(1,128)S(1)}, u32[]{:S(2)}, u32[]{:S(2)}) collective-permute-start(f32[8,8,1,128]{3,2,1,0:T(1,128)} %get-tuple-element.76), channel_id=1, source_target_pairs={{16,0},{32,16},{48,32},{64,48},{80,64},{96,80},{112,96},{128,112},... | collective-permute-start | bytes 98312 | tf_op jit(solution)/shard_map/ppermute | solution.py:21
  84.0 14.6 %collective-permute-start.25 = (f32[8,8,1,128]{3,2,1,0:T(1,128)}, f32[8,8,1,128]{3,2,1,0:T(1,128)S(1)}, u32[]{:S(2)}, u32[]{:S(2)}) collective-permute-start(f32[8,8,1,128]{3,2,1,0:T(1,128)} %get-tuple-element.75), channel_id=1, source_target_pairs={{0,16},{16,32},{32,48},{48,64},{64,80},{80,96},{96,112},{112,128},... | collective-permute-start | bytes 98312 | tf_op jit(solution)/shard_map/ppermute | solution.py:19
  91.6 13.6 %collective-permute-start.10 = (f32[8,8,10,1]{3,2,1,0:T(8,128)S(1)}, f32[8,8,10,1]{3,2,1,0:T(8,128)S(1)}, u32[]{:S(2)}, u32[]{:S(2)}) collective-permute-start(f32[8,8,10,1]{3,2,1,0:T(8,128)S(1)} %get-tuple-element.61), channel_id=1, source_target_pairs={{0,1},{1,2},{2,3},{3,4},{4,5},{5,6},{6,7},{7,8},{8,9},{9,10},{10,1... | collective-permute-start | bytes 7688 | tf_op jit(solution)/shard_map/ppermute | solution.py:19
  96.6 10.5 %collective-permute-start.11 = (f32[8,8,10,1]{3,2,1,0:T(8,128)S(1)}, f32[8,8,10,1]{3,2,1,0:T(8,128)S(1)}, u32[]{:S(2)}, u32[]{:S(2)}) collective-permute-start(f32[8,8,10,1]{3,2,1,0:T(8,128)S(1)} %get-tuple-element.62), channel_id=1, source_target_pairs={{1,0},{2,1},{3,2},{4,3},{5,4},{6,5},{7,6},{8,7},{9,8},{10,9},{11,1... | collective-permute-start | bytes 7688 | tf_op jit(solution)/shard_map/ppermute | solution.py:21
  99.3 13.3 %collective-permute-start.26 = (f32[8,8,10,1]{3,2,1,0:T(8,128)S(1)}, f32[8,8,10,1]{3,2,1,0:T(8,128)S(1)}, u32[]{:S(2)}, u32[]{:S(2)}) collective-permute-start(f32[8,8,10,1]{3,2,1,0:T(8,128)S(1)} %get-tuple-element.58), channel_id=1, source_target_pairs={{1,0},{2,1},{3,2},{4,3},{5,4},{6,5},{7,6},{8,7},{9,8},{10,9},{11,1... | collective-permute-start | bytes 7688 | tf_op jit(solution)/shard_map/ppermute | solution.py:21
  101.3 7.3 %copy-start.13 = (f32[7,8,128]{2,1,0:T(8,128)S(1)}, f32[7,8,128]{2,1,0:T(8,128)}, u32[]{:S(2)}) copy-start(f32[7,8,128]{2,1,0:T(8,128)} %copy-done.12) | copy-start | bytes 86020
  101.3 7.3 %copy-start.16 = (f32[7,8,128]{2,1,0:T(8,128)S(1)}, f32[7,8,128]{2,1,0:T(8,128)}, u32[]{:S(2)}) copy-start(f32[7,8,128]{2,1,0:T(8,128)} %copy-done.15) | copy-start | bytes 86020
  101.3 11.4 %collective-permute-start.27 = (f32[8,8,10,1]{3,2,1,0:T(8,128)S(1)}, f32[8,8,10,1]{3,2,1,0:T(8,128)S(1)}, u32[]{:S(2)}, u32[]{:S(2)}) collective-permute-start(f32[8,8,10,1]{3,2,1,0:T(8,128)S(1)} %get-tuple-element.57), channel_id=1, source_target_pairs={{0,1},{1,2},{2,3},{3,4},{4,5},{5,6},{6,7},{7,8},{8,9},{9,10},{10,1... | collective-permute-start | bytes 7688 | tf_op jit(solution)/shard_map/ppermute | solution.py:19
  108.6 0.9 copy-start.4
  108.6 1.0 copy-start.6
  108.6 1.0 copy-start.10
  108.7 1.0 copy-start.19
  108.7 1.0 copy-start.21
  109.7 3.0 %copy-start.7 = (f32[7,8,8,128]{3,2,1,0:T(8,128)S(1)}, f32[7,8,8,128]{3,2,1,0:T(8,128)}, u32[]{:S(2)}) copy-start(f32[7,8,8,128]{3,2,1,0:T(8,128)} %get-tuple-element.77) | copy-start | bytes 688132
  109.7 3.0 %copy-start.8 = (f32[7,8,8,128]{3,2,1,0:T(8,128)S(1)}, f32[7,8,8,128]{3,2,1,0:T(8,128)}, u32[]{:S(2)}) copy-start(f32[7,8,8,128]{3,2,1,0:T(8,128)} %get-tuple-element.78) | copy-start | bytes 688132
  109.7 3.0 %copy-start.39 = (f32[8,8,1,128]{3,2,1,0:T(1,128)S(1)}, f32[8,8,1,128]{3,2,1,0:T(1,128)}, u32[]{:S(2)}) copy-start(f32[8,8,1,128]{3,2,1,0:T(1,128)} %copy-done.38) | copy-start | bytes 98308
  109.7 3.0 %copy-start.41 = (f32[8,8,1,128]{3,2,1,0:T(1,128)S(1)}, f32[8,8,1,128]{3,2,1,0:T(1,128)}, u32[]{:S(2)}) copy-start(f32[8,8,1,128]{3,2,1,0:T(1,128)} %copy-done.40) | copy-start | bytes 98308
  113.5 0.8 copy-start.28
  113.5 0.8 copy-start.29
  113.5 0.8 copy-start.30
  113.5 1.1 copy-start.24
  113.9 1.0 copy-start.22
  114.3 0.8 copy-start.43
  115.9 146.0 %collective-permute-start.12 = (f32[8,8,1,128]{3,2,1,0:T(1,128)S(1)}, f32[8,8,1,128]{3,2,1,0:T(1,128)S(1)}, u32[]{:S(2)}, u32[]{:S(2)}) collective-permute-start(f32[8,8,1,128]{3,2,1,0:T(1,128)S(1)} %get-tuple-element.79), channel_id=1, source_target_pairs={{0,16},{16,32},{32,48},{48,64},{64,80},{80,96},{96,112},{112,128},... | collective-permute-start | bytes 98312 | tf_op jit(solution)/shard_map/ppermute | solution.py:19
  121.1 140.8 %collective-permute-start.13 = (f32[8,8,1,128]{3,2,1,0:T(1,128)S(1)}, f32[8,8,1,128]{3,2,1,0:T(1,128)S(1)}, u32[]{:S(2)}, u32[]{:S(2)}) collective-permute-start(f32[8,8,1,128]{3,2,1,0:T(1,128)S(1)} %get-tuple-element.80), channel_id=1, source_target_pairs={{16,0},{32,16},{48,32},{64,48},{80,64},{96,80},{112,96},{128,112},... | collective-permute-start | bytes 98312 | tf_op jit(solution)/shard_map/ppermute | solution.py:21
  262.2 8.2 %collective-permute-start.14 = (f32[8,8,10,1]{3,2,1,0:T(8,128)S(1)}, f32[8,8,10,1]{3,2,1,0:T(8,128)S(1)}, u32[]{:S(2)}, u32[]{:S(2)}) collective-permute-start(f32[8,8,10,1]{3,2,1,0:T(8,128)S(1)} %get-tuple-element.59), channel_id=1, source_target_pairs={{0,1},{1,2},{2,3},{3,4},{4,5},{5,6},{6,7},{7,8},{8,9},{9,10},{10,1... | collective-permute-start | bytes 7688 | tf_op jit(solution)/shard_map/ppermute | solution.py:19
  264.3 10.5 %collective-permute-start.15 = (f32[8,8,10,1]{3,2,1,0:T(8,128)S(1)}, f32[8,8,10,1]{3,2,1,0:T(8,128)S(1)}, u32[]{:S(2)}, u32[]{:S(2)}) collective-permute-start(f32[8,8,10,1]{3,2,1,0:T(8,128)S(1)} %get-tuple-element.60), channel_id=1, source_target_pairs={{1,0},{2,1},{3,2},{4,3},{5,4},{6,5},{7,6},{8,7},{9,8},{10,9},{11,1... | collective-permute-start | bytes 7688 | tf_op jit(solution)/shard_map/ppermute | solution.py:21
  267.0 8.5 %copy-start.14 = (f32[7,8,128]{2,1,0:T(8,128)S(1)}, f32[7,8,128]{2,1,0:T(8,128)}, u32[]{:S(2)}) copy-start(f32[7,8,128]{2,1,0:T(8,128)} %copy-done.12) | copy-start | bytes 86020
  267.1 8.5 %copy-start.17 = (f32[7,8,128]{2,1,0:T(8,128)S(1)}, f32[7,8,128]{2,1,0:T(8,128)}, u32[]{:S(2)}) copy-start(f32[7,8,128]{2,1,0:T(8,128)} %copy-done.15) | copy-start | bytes 86020
  (8 other events, 5.8 us)
where the time goes:
time: 281 us; the launch traced here: 277 us
  blocking collectives  139 us (49%)
  starting transfers between devices  93.1 us (33%)
  waiting for transfers between devices  18.5 us (7%)
  other arithmetic  12.4 us (4%)
  local copies, waits for them, and re-layouts  11.4 us (4%)
    psum x1, blocking collectives, per_device(): weight_sum, bias_sum = lax.psum((weight_part, bias_part), ('gx', 'gy'))  139 us
    ppermute x14, starting transfers between devices, with_halo(): lax.ppermute(tail, axis, [(i, (i + 1) % count) for i in range(ends)])  64 us
    ppermute x14, starting transfers between devices, with_halo(): lax.ppermute(head, axis, [((i + 1) % count, i) for i in range(ends)])  29.1 us
    ppermute x14, waiting for transfers between devices, with_halo(): lax.ppermute(head, axis, [((i + 1) % count, i) for i in range(ends)])  12.9 us
    ppermute x14, waiting for transfers between devices, with_halo(): lax.ppermute(tail, axis, [(i, (i + 1) % count) for i in range(ends)])  5.7 us
  transfers between devices with their start and end apart: 28, of which 8 were waited for; matrix products, arithmetic and copies ran while one was open for 4% of the time, Pallas kernels for 0%

commit v1 on v0

v1 whole, which is shorter than its diff:
```python
import math

import jax
import jax.numpy as jnp
from jax import lax
from jax.experimental import pallas as pl
from jax.experimental.pallas import tpu as pltpu
from jax.sharding import PartitionSpec as P

F32 = jnp.float32
BF16 = jnp.bfloat16
MESH = pl.DeviceIdType.MESH
ITERS = 3
FROM_PLUS, FROM_MINUS = 0, 1
H_PART, G_PART = 0, 1


def iota(shape, dim):
    return lax.broadcasted_iota(jnp.int32, shape, dim)


def make_kernel(zs, chans, feats, gx, gy, inner, factor):
    outer = gx // inner
    nx, ny = 8, 128

    def kernel(
        feat_hbm, weight_ref, bias_ref, probs_hbm, cot_hbm,
        out_hbm, gw_ref, gb_ref,
        feat, h_all, g_all, g_out, kap, cen, act, inv, kgrad, dlow, bias_acc, wide,
        send_x, recv_x, send_y, recv_y, sum_a, sum_b, sum_c,
        local_sem, sx_sem, rx_sem, sy_sem, ry_sem, sa_sem, ra_sem, sb_sem, rb_sem, sc_sem, rc_sem,
    ):
        me_x, me_y = lax.axis_index("gx"), lax.axis_index("gy")
        me_in, me_out = lax.rem(me_x, inner), lax.div(me_x, inner)
        right, left = lax.rem(me_x + 1, gx), lax.rem(me_x + gx - 1, gx)
        up, down = lax.rem(me_y + 1, gy), lax.rem(me_y + gy - 1, gy)

        loads = [
            pltpu.make_async_copy(probs_hbm, h_all.at[0, pl.ds(1, zs)], local_sem.at[0]),
            pltpu.make_async_copy(cot_hbm, g_all.at[0, pl.ds(1, zs)], local_sem.at[1]),
            pltpu.make_async_copy(feat_hbm, feat, local_sem.at[2]),
        ]
        for load in loads:
            load.start()

        partners_a = [(me_x, lax.rem(me_y + d, gy)) for d in range(1, gy)]
        partners_b = [(me_out * inner + lax.rem(me_in + d, inner), me_y) for d in range(1, inner)]
        partners_c = [(lax.rem(me_out + d, outer) * inner + me_in, me_y) for d in range(1, outer)]
        greeted = [(left, me_y), (right, me_y)] + partners_a + partners_b + partners_c
        barrier = pltpu.get_barrier_semaphore()
        for partner in greeted:
            pl.semaphore_signal(barrier, inc=1, device_id=partner, device_id_type=MESH)

        blank = jnp.zeros((chans, nx, ny), F32)
        for field in (h_all, g_all):
            for step in range(ITERS):
                field[step, 0] = blank
                field[step, zs + 1] = blank
        kap[0] = jnp.zeros((6, nx, ny), F32)
        kap[zs + 1] = jnp.zeros((6, nx, ny), F32)

        spread = (iota((feats, feats * nx), 1) >> 3) == iota((feats, feats * nx), 0)
        same_x = (iota((6 * nx, feats * nx), 1) & 7) == (iota((6 * nx, feats * nx), 0) & 7)
        weight = weight_ref[...].astype(F32)
        rows = jnp.concatenate(
            [jnp.broadcast_to(weight[k : k + 1, :], (nx, feats)) for k in range(6)], axis=0
        )
        tall = jnp.dot(
            rows.astype(BF16), spread.astype(F32).astype(BF16), preferred_element_type=F32
        )
        wide[...] = jnp.where(same_x, tall, 0.0).astype(BF16)

        row_at = iota((chans, nx, ny), 1)
        lane_at = iota((chans, nx, ny), 2)
        lane = iota((nx, ny), 1)
        has_right, has_left = me_x < gx - 1, me_x > 0
        has_up, has_down = me_y < gy - 1, me_y > 0

        def stage_rows(rnd, part, z, for_right, for_left):
            send_x[rnd, FROM_MINUS, part, z] = jnp.where(has_right, for_right, 0.0)
            send_x[rnd, FROM_PLUS, part, z] = jnp.where(has_left, for_left, 0.0)

        def lanes_of(tile, first, value, source):
            for c in range(chans):
                column = jnp.broadcast_to(value[c][:, source : source + 1], (nx, ny))
                tile = jnp.where(lane == first + c, column, tile)
            return tile

        def stage_lanes(rnd, z, h, p2, p3):
            tile = jnp.zeros((nx, ny), F32)
            ahead = lanes_of(lanes_of(tile, 0, h, ny - 1), chans, p2, ny - 1)
            back = lanes_of(lanes_of(tile, 0, h, 0), chans, p3, 0)
            send_y[rnd, FROM_MINUS, z] = jnp.where(has_up, ahead, 0.0)
            send_y[rnd, FROM_PLUS, z] = jnp.where(has_down, back, 0.0)

        def rim_lanes(rnd, direction, part, z):
            tile = recv_y[rnd, direction, z]
            first = part * chans
            return jnp.stack(
                [jnp.broadcast_to(tile[:, first + c : first + c + 1], (nx, ny)) for c in range(chans)]
            )

        def copies_x(rnd, part):
            return [
                pltpu.make_async_remote_copy(
                    src_ref=send_x.at[rnd, direction, part],
                    dst_ref=recv_x.at[rnd, direction, part],
                    send_sem=sx_sem.at[rnd, direction, part],
                    recv_sem=rx_sem.at[rnd, direction, part],
                    device_id=(target, me_y),
                    device_id_type=MESH,
                )
                for direction, target in ((FROM_MINUS, right), (FROM_PLUS, left))
            ]

        def copies_y(rnd):
            return [
                pltpu.make_async_remote_copy(
                    src_ref=send_y.at[rnd, direction],
                    dst_ref=recv_y.at[rnd, direction],
                    send_sem=sy_sem.at[rnd, direction],
                    recv_sem=ry_sem.at[rnd, direction],
                    device_id=(me_x, target),
                    device_id_type=MESH,
                )
                for direction, target in ((FROM_MINUS, up), (FROM_PLUS, down))
            ]

        def around(rnd, z):
            h = h_all[rnd, z + 1]
            beside = [
                jnp.where(row_at == nx - 1, recv_x[rnd, FROM_PLUS, H_PART, z], pltpu.roll(h, nx - 1, 1)),
                jnp.where(row_at == 0, recv_x[rnd, FROM_MINUS, H_PART, z], pltpu.roll(h, 1, 1)),
                jnp.where(lane_at == ny - 1, rim_lanes(rnd, FROM_PLUS, H_PART, z), pltpu.roll(h, ny - 1, 2)),
                jnp.where(lane_at == 0, rim_lanes(rnd, FROM_MINUS, H_PART, z), pltpu.roll(h, 1, 2)),
                h_all[rnd, z + 2],
                h_all[rnd, z],
            ]
            return h, beside

        def forward(rnd, z):
            h, beside = around(rnd, z)
            result = cen[z] * h
            for k in range(6):
                result = result + kap[z + 1, k] * beside[k]
            return result

        def backward(rnd, z):
            g = g_all[rnd, z + 1]
            p0, p1, p2, p3 = (kap[z + 1, k] * g for k in range(4))
            result = cen[z] * g
            result = result + jnp.where(
                row_at == 0, recv_x[rnd, FROM_MINUS, G_PART, z], pltpu.roll(p0, 1, 1)
            )
            result = result + jnp.where(
                row_at == nx - 1, recv_x[rnd, FROM_PLUS, G_PART, z], pltpu.roll(p1, nx - 1, 1)
            )
            result = result + jnp.where(
                lane_at == 0, rim_lanes(rnd, FROM_MINUS, G_PART, z), pltpu.roll(p2, 1, 2)
            )
            result = result + jnp.where(
                lane_at == ny - 1, rim_lanes(rnd, FROM_PLUS, G_PART, z), pltpu.roll(p3, ny - 1, 2)
            )
            result = result + kap[z, 4] * g_all[rnd, z] + kap[z + 2, 5] * g_all[rnd, z + 2]
            return result

        def stage(rnd, z, h, g):
            k = kap[z + 1]
            stage_rows(rnd, H_PART, z, h[:, nx - 1 :, :], h[:, :1, :])
            stage_rows(
                rnd, G_PART, z,
                k[0][None, nx - 1 :, :] * g[:, nx - 1 :, :], k[1][None, :1, :] * g[:, :1, :],
            )
            stage_lanes(rnd, z, h, k[2] * g, k[3] * g)

        def over_z(body):
            def run(z, carry):
                body(z)
                return carry

            lax.fori_loop(0, zs, run, 0)

        for load in loads:
            load.wait()
        biases = [bias_ref[k] for k in range(6)]

        def head(z):
            logits = jnp.dot(wide[...], feat[z], preferred_element_type=F32)
            active = [jax.nn.sigmoid(logits[k * nx : (k + 1) * nx] + biases[k]) for k in range(6)]
            summed = active[0]
            for k in range(1, 6):
                summed = summed + active[k]
            inverse = 1.0 / (summed + 1.0)
            total = jnp.zeros((nx, ny), F32)
            for k in range(6):
                coupling = active[k] * inverse
                act[z, k] = active[k]
                kap[z + 1, k] = coupling
                total = total + coupling
            inv[z] = inverse
            cen[z] = 1.0 - total
            stage(0, z, h_all[0, z + 1], g_all[0, z + 1])

        over_z(head)
        pl.semaphore_wait(barrier, len(greeted))

        pending = []

        def launch(rnd):
            copies = copies_y(rnd) + copies_x(rnd, H_PART) + copies_x(rnd, G_PART)
            for copy in copies:
                copy.start()
            pending.extend(copies)
            return copies

        for rnd in range(ITERS - 1):
            for copy in launch(rnd):
                copy.wait_recv()

            def advance(z, rnd=rnd):
                h, g = forward(rnd, z), backward(rnd, z)
                h_all[rnd + 1, z + 1] = h
                g_all[rnd + 1, z + 1] = g
                stage(rnd + 1, z, h, g)

            over_z(advance)
        last = launch(ITERS - 1)

        def terms(z, rounds):
            parts = [jnp.zeros((nx, ny), F32) for _ in range(7)]
            for rnd in rounds:
                g = g_all[ITERS - 1 - rnd, z + 1]
                h, beside = around(rnd, z)
                for k in range(6):
                    parts[k] = parts[k] + jnp.sum(g * beside[k], 0)
                parts[6] = parts[6] + jnp.sum(g * h, 0)
            return parts

        def early(z):
            parts = terms(z, range(ITERS - 1))
            for k in range(7):
                kgrad[z, k] = parts[k]

        over_z(early)
        bias_acc[...] = jnp.zeros((6, nx, ny), F32)
        for copy in last:
            copy.wait_recv()

        def late(z):
            parts = terms(z, [ITERS - 1])
            inner_sum = jnp.zeros((nx, ny), F32)
            effective = []
            centre_grad = parts[6] + kgrad[z, 6]
            for k in range(6):
                value = parts[k] + kgrad[z, k] - centre_grad
                effective.append(value)
                inner_sum = inner_sum + value * kap[z + 1, k]
            pieces = []
            for k in range(6):
                active = act[z, k]
                slope = (effective[k] - inner_sum) * inv[z] * active * (1.0 - active)
                bias_acc[k] += slope
                pieces.append(slope)
            dlow[z] = jnp.concatenate(pieces, axis=0).astype(BF16)

        over_z(late)

        total = jnp.zeros((6 * nx, feats * nx), F32)
        for z in range(0, zs, 2):
            total = total + lax.dot_general(
                jnp.concatenate([dlow[z], dlow[z + 1]], axis=1),
                jnp.concatenate([feat[z], feat[z + 1]], axis=1),
                (((1,), (1,)), ((), ())),
                preferred_element_type=F32,
            )
        total = jnp.where(same_x, total, 0.0)
        by_k = jnp.concatenate(
            [jnp.sum(total[k * nx : (k + 1) * nx], 0, keepdims=True) for k in range(6)]
            + [jnp.zeros((2, feats * nx), F32)],
            axis=0,
        )
        fold = ((iota((feats * nx, 2 * feats), 0) >> 3) == iota((feats * nx, 2 * feats), 1)).astype(F32)
        by_f = jnp.dot(by_k, fold, precision=lax.Precision.HIGHEST, preferred_element_type=F32)
        lane_row = iota((1, ny), 1)
        payload = [
            jnp.where(
                lane_row < feats,
                by_f[2 * r : 2 * r + 1],
                pltpu.roll(by_f[2 * r + 1 : 2 * r + 2], feats, 1),
            )
            for r in range(3)
        ]
        bias_row = jnp.zeros((1, ny), F32)
        for k in range(6):
            amount = jnp.sum(jnp.sum(bias_acc[k], 0, keepdims=True), 1, keepdims=True)
            bias_row = jnp.where(lane_row == k, amount, bias_row)
        payload = jnp.concatenate(payload + [bias_row], axis=0)

        def exchange(buffer, me, partners, positions, send_sem, recv_sem, value):
            buffer[me] = value
            copies = []
            for d, (partner, position) in enumerate(zip(partners, positions)):
                copy = pltpu.make_async_remote_copy(
                    src_ref=buffer.at[me],
                    dst_ref=buffer.at[me],
                    send_sem=send_sem.at[d],
                    recv_sem=recv_sem.at[d],
                    device_id=partner,
                    device_id_type=MESH,
                )
                copy.start()
                copies.append(copy)
            pending.extend(copies)
            return copies

        def gather(buffer, copies, count):
            for copy in copies:
                copy.wait_recv()
            value = buffer[0]
            for i in range(1, count):
                value = value + buffer[i]
            return value

        first = exchange(sum_a, me_y, partners_a, partners_a, sa_sem, ra_sem, payload)

        def finish(z):
            g_out[z] = backward(ITERS - 1, z)

        over_z(finish)
        store = pltpu.make_async_copy(g_out, out_hbm, local_sem.at[3])
        store.start()

        value = gather(sum_a, first, gy)
        second = exchange(sum_b, me_in, partners_b, partners_b, sb_sem, rb_sem, value)
        value = gather(sum_b, second, inner)
        third = exchange(sum_c, me_out, partners_c, partners_c, sc_sem, rc_sem, value)
        value = gather(sum_c, third, outer) * factor
        for k in range(6):
            row = value[k // 2 : k // 2 + 1]
            if k % 2:
                row = pltpu.roll(row, feats, 1)
            gw_ref[k : k + 1, :] = row[:, :feats]
        gb_ref[...] = value[3:4, :6]
        for copy in pending:
            copy.wait_send()
        store.wait()

    return kernel


def inner_of(gx):
    return 8 if gx == 64 else 2


def per_device(features, head_weight, head_bias, probs, cotangent):
    zs, feats, nx, ny = features.shape
    chans = probs.shape[1]
    gx, gy = lax.axis_size("gx"), lax.axis_size("gy")
    inner = inner_of(gx)
    outer = gx // inner
    factor = 1.0 / math.sqrt(zs * nx * ny * gx * gy)
    field = (zs + 2, chans, nx, ny)
    dma = pltpu.SemaphoreType.DMA
    rim_x = (ITERS, 2, 2, zs, chans, 1, ny)
    rim_y = (ITERS, 2, zs, nx, ny)
    hbm = pl.BlockSpec(memory_space=pltpu.HBM)
    vmem = pl.BlockSpec(memory_space=pltpu.VMEM)
    grad_probs, grad_weight, grad_bias = pl.pallas_call(
        make_kernel(zs, chans, feats, gx, gy, inner, factor),
        out_shape=(
            jax.ShapeDtypeStruct(probs.shape, F32),
            jax.ShapeDtypeStruct((6, feats), F32),
            jax.ShapeDtypeStruct((1, 6), F32),
        ),
        in_specs=[hbm, vmem, pl.BlockSpec(memory_space=pltpu.SMEM), hbm, hbm],
        out_specs=(hbm, vmem, vmem),
        scratch_shapes=[
            pltpu.VMEM((zs, feats * nx, ny), BF16),
            pltpu.VMEM((ITERS,) + field, F32),
            pltpu.VMEM((ITERS,) + field, F32),
            pltpu.VMEM((zs, chans, nx, ny), F32),
            pltpu.VMEM((zs + 2, 6, nx, ny), F32),
            pltpu.VMEM((zs, nx, ny), F32),
            pltpu.VMEM((zs, 6, nx, ny), F32),
            pltpu.VMEM((zs, nx, ny), F32),
            pltpu.VMEM((zs, 7, nx, ny), F32),
            pltpu.VMEM((zs, 6 * nx, ny), BF16),
            pltpu.VMEM((6, nx, ny), F32),
            pltpu.VMEM((6 * nx, feats * nx), BF16),
            pltpu.VMEM(rim_x, F32),
            pltpu.VMEM(rim_x, F32),
            pltpu.VMEM(rim_y, F32),
            pltpu.VMEM(rim_y, F32),
            pltpu.VMEM((gy, 4, ny), F32),
            pltpu.VMEM((inner, 4, ny), F32),
            pltpu.VMEM((outer, 4, ny), F32),
            dma((4,)),
            dma((ITERS, 2, 2)),
            dma((ITERS, 2, 2)),
            dma((ITERS, 2)),
            dma((ITERS, 2)),
            dma((gy - 1,)),
            dma((gy - 1,)),
            dma((inner - 1,)),
            dma((inner - 1,)),
            dma((outer - 1,)),
            dma((outer - 1,)),
        ],
        compiler_params=pltpu.CompilerParams(
            collective_id=0, has_side_effects=True, vmem_limit_bytes=63 * 1024 * 1024
        ),
        name="spread_backward",
    )(features.reshape(zs, feats * nx, ny), head_weight, head_bias, probs, cotangent)
    return grad_probs, grad_weight, grad_bias.reshape(6)


def solution(mesh):
    spec = P(None, None, "gx", "gy")
    return jax.shard_map(
        per_device,
        mesh=mesh,
        in_specs=(spec, P(), P(), spec, spec),
        out_specs=(spec, P(), P()),
        check_vma=False,
    )
```

time: 281 us -> 60.7 us (0.22); the launches traced: 277 us -> 60.5 us
  blocking collectives: 139 us -> 0 us
  starting transfers between devices: 93.1 us -> 0 us
  Pallas kernels: 0 us -> 57 us
  waiting for transfers between devices: 18.5 us -> 0 us
  other arithmetic: 12.4 us -> 0 us
  local copies, waits for them, and re-layouts: 11.4 us -> 2.86 us
    psum x1 -> x0, blocking collectives: 139 us -> none  [per_device(): weight_sum, bias_sum = lax.psum((weight_part, bias_part), ('gx', 'gy'))]
    ppermute x28 -> x0, starting transfers between devices: 93.1 us -> none  [the longest x14 64 us: with_halo(): lax.ppermute(tail, axis, [(i, (i + 1) % count) for i in range(ends)])]
    pallas_call x0 -> x1, Pallas kernels: none -> 57 us  [per_device(): pl.pallas_call(make_kernel(zs, chans, feats, gx, gy, inner, factor), out_...]
    ppermute x28 -> x0, waiting for transfers between devices: 18.5 us -> none  [the longest x14 12.9 us: with_halo(): lax.ppermute(head, axis, [((i + 1) % count, i) for i in range(ends)])]
    slice x25 -> x0, local copies, waits for them, and re-layouts: 4.67 us -> none  [the longest x14 2.9 us: with_halo(): lax.slice_in_dim(cells, cells.shape[dim] - width, cells.shape[dim], axis=...]
    concatenate x10 -> x0, other arithmetic: 4.44 us -> none  [with_halo(): jnp.concatenate([lax.ppermute(tail, axis, [(i, (i + 1) % count) for i in...]
    reduce_sum x5 -> x0, other arithmetic: 3.82 us -> none  [the longest x3 3.35 us: local_terms(): jnp.sum(grad_field * beside[direction], 1)]
  transfers between devices with their start and end apart: 28 -> 0, of which waited for: 8 -> 0; matrix products, arithmetic and copies ran while one was open for 4% -> 0% of each run, Pallas kernels for 0% -> 0%
where the time goes in v1:
time: 60.7 us; the launch traced here: 60.5 us
  Pallas kernels  57 us (94%)
  local copies, waits for them, and re-layouts  2.86 us (5%)
  between operations  0.65 us (1%)
    pallas_call x1, Pallas kernels, per_device(): pl.pallas_call(make_kernel(zs, chans, feats, gx, gy, inner, factor), out_...  57 us
    unnamed x7, local copies, waits for them, and re-layouts  2.86 us

profile of v1, /device:TPU:1, one launch (start us, length us, event | category | flops | bytes accessed | tf_op | source)
XLA Modules:
  0.0 60.5 jit_solution(6246910712184390849)
XLA Ops:
  0.6 57.0 %spread_backward.1 = (f32[8,8,8,128]{3,2,1,0:T(8,128)}, f32[6,64]{1,0:T(8,128)}, f32[1,6]{1,0:T(1,128)}) custom-call(bf16[8,512,128]{2,1,0:T(8,128)(2,1)} %bitcast.2, bf16[6,64]{1,0:T(8,128)(2,1)} %weight_ref.1, f32[6]{0:T(128)} %bias_ref.1, f32[8,8,8,128]{3,2,1,0:T(8,128)} %probs_hbm.1, f32[8,8,8,128]{3,2,1,0:T(8,128)} %cot_hbm.1), custom_call_target="tpu_custom_call" | custom-call | tf_op jit(solution)/shard_map/spread_backward/pallas_call | solution.py:368
  57.6 0.0 copy-start
  57.6 1.7 %copy.11 = f32[8,8,8,128]{3,2,1,0:T(8,128)} copy(f32[8,8,8,128]{3,2,1,0:T(8,128)} %get-tuple-element.12) | data formatting | bytes 524288
  59.3 0.0 copy-done
  59.3 0.0 copy-start.1
  59.3 0.6 copy.12
  59.9 0.1 copy-done.1
  60.0 0.5 copy.13
Async XLA Ops:
  57.6 1.7 %copy-start = (f32[6,64]{1,0:T(8,128)S(1)}, f32[6,64]{1,0:T(8,128)}, u32[]{:S(2)}) copy-start(f32[6,64]{1,0:T(8,128)} %get-tuple-element.13) | copy-start | bytes 4612
  59.3 0.7 %copy-start.1 = (f32[1,6]{1,0:T(1,128)S(1)}, f32[1,6]{1,0:T(1,128)}, u32[]{:S(2)}) copy-start(f32[1,6]{1,0:T(1,128)} %get-tuple-element.8) | copy-start | bytes 76

commit v2 on v1

v2 whole, which is shorter than its diff:
```python
import math

import jax
import jax.numpy as jnp
from jax import lax
from jax.experimental import pallas as pl
from jax.experimental.pallas import tpu as pltpu
from jax.sharding import PartitionSpec as P

F32 = jnp.float32
BF16 = jnp.bfloat16
MESH = pl.DeviceIdType.MESH
ITERS = 3
NX, NY = 8, 128
RING = 16
EDGE = 16
LOW, HIGH = 3, 12
SIDES = [(dx, dy) for dx in (1, -1, 0) for dy in (0, 1, -1) if dx or dy]


def iota(shape, dim):
    return lax.broadcasted_iota(jnp.int32, shape, dim)


def rows_of(dx):
    if dx == 0:
        return pl.ds(0, NX), pl.ds(0, NX)
    if dx > 0:
        return pl.ds(NX - 3, 3), pl.ds(RING - 3, 3)
    return pl.ds(0, 3), pl.ds(NX, 3)


def make_kernel(zs, chans, feats, gx, gy, inner, factor):
    outer = gx // inner
    inside = pl.ds(1, zs)

    def kernel(
        feat_hbm, weight_ref, bias_ref, probs_hbm, cot_hbm,
        out_hbm, sum_ref,
        feat, hs, gs, g_out, kap, kst, act, inv, dlow, bias_acc, wide, expand,
        sf, sk, flat, sum_a, sum_b, sum_c,
        local_sem, row_send, row_recv, strip_send, strip_recv,
        sa_sem, ra_sem, sb_sem, rb_sem, sc_sem, rc_sem,
    ):
        me_x, me_y = lax.axis_index("gx"), lax.axis_index("gy")
        me_in, me_out = lax.rem(me_x, inner), lax.div(me_x, inner)

        def at(dx, dy):
            return lax.rem(me_x + dx + gx, gx), lax.rem(me_y + dy + gy, gy)

        partners_a = [(me_x, lax.rem(me_y + d, gy)) for d in range(1, gy)]
        partners_b = [(me_out * inner + lax.rem(me_in + d, inner), me_y) for d in range(1, inner)]
        partners_c = [(lax.rem(me_out + d, outer) * inner + me_in, me_y) for d in range(1, outer)]
        greeted = [at(dx, dy) for dx, dy in SIDES if dx] + partners_a + partners_b + partners_c
        barrier = pltpu.get_barrier_semaphore()
        for partner in greeted:
            pl.semaphore_signal(barrier, inc=1, device_id=partner, device_id_type=MESH)

        fields_in = [
            pltpu.make_async_copy(source, field.at[0, inside, pl.ds(0, chans), pl.ds(0, NX)], local_sem.at[i])
            for i, (source, field) in enumerate(((probs_hbm, hs), (cot_hbm, gs)))
        ]
        feats_in = [
            pltpu.make_async_copy(feat_hbm.at[z], feat.at[z], local_sem.at[2 + z]) for z in range(zs)
        ]
        for load in fields_in + feats_in:
            load.start()

        for field in (hs, gs):
            for step in range(ITERS):
                for z in (0, zs + 1):
                    field[step, z] = jnp.zeros((chans + 1, RING, NY), F32)
        for coefs in (kap, kst):
            for z in (0, zs + 1):
                coefs[z] = jnp.zeros((7, RING, NY), F32)

        spread = (iota((feats, feats * NX), 1) >> 3) == iota((feats, feats * NX), 0)
        same_x = (iota((6 * NX, feats * NX), 1) & 7) == (iota((6 * NX, feats * NX), 0) & 7)
        weight = weight_ref[...].astype(F32)
        rows = jnp.concatenate(
            [jnp.broadcast_to(weight[k : k + 1, :], (NX, feats)) for k in range(6)], axis=0
        )
        tall = jnp.dot(
            rows.astype(BF16), spread.astype(F32).astype(BF16), preferred_element_type=F32
        )
        wide[...] = jnp.where(same_x, tall, 0.0).astype(BF16)
        here, there = iota((NY, 6 * NY), 0), iota((NY, 6 * NY), 1)
        expand[...] = (((here >> 4) == (there >> 7)) & ((here & 15) == (there & 15))).astype(F32)

        lane = iota((NX, NY), 1)
        lane_j = lane & (EDGE - 1)
        ring_lane = iota((RING, NY), 1)
        ring_j = ring_lane & (EDGE - 1)
        ring_row = iota((RING, NY), 0)
        has_right, has_left = me_x < gx - 1, me_x > 0
        has_up, has_down = me_y < gy - 1, me_y > 0

        def packed(values):
            tile = jnp.zeros((NX, NY), F32)
            for i, value in enumerate(values):
                tile = jnp.where((lane >> 4) == i, pltpu.roll(value, i * EDGE + 4, 1), tile)
            return jnp.where(lane_j < 8, tile, 0.0)

        def unpacked(own, low, high):
            seen = (
                (ring_row < NX) | ((ring_row < NX + 4) & has_right) | ((ring_row >= NX + 4) & has_left)
            )
            low = jnp.where(has_down, low, 0.0)
            high = jnp.where(has_up, high, 0.0)
            near = jnp.where(ring_j < 4, low, own)
            far = pltpu.roll(jnp.where(ring_j < 4, own, high), 8, 1)
            return jnp.where(seen, jnp.where(ring_j < 8, near, far), 0.0)

        def over_z(body):
            def run(z, carry):
                body(z)
                return carry

            lax.fori_loop(0, zs, run, 0, unroll=True)

        def remote(source, target, send_sem, recv_sem, device):
            return pltpu.make_async_remote_copy(
                src_ref=source, dst_ref=target, send_sem=send_sem, recv_sem=recv_sem,
                device_id=device, device_id_type=MESH,
            )

        pending, arriving = [], []

        def send(copies):
            for copy in copies:
                copy.start()
            pending.extend(copies)
            arriving.extend(copies)

        def row_copies(which, view):
            return [
                remote(
                    view(rows_of(dx)[0]), view(rows_of(dx)[1]),
                    row_send.at[which, i], row_recv.at[which, i], at(dx, 0),
                )
                for i, dx in enumerate((1, -1))
            ]

        def strip_copies(which, view):
            return [
                remote(
                    view(0, rows_of(dx)[0]), view((0, 1, 2)[dy], rows_of(dx)[1]),
                    strip_send.at[which, i], strip_recv.at[which, i], at(dx, dy),
                )
                for i, (dx, dy) in enumerate(SIDES)
            ]

        for load in fields_in:
            load.wait()

        def pack_fields(z):
            sf[0, 0, z, :NX] = packed([hs[0, z + 1, c, :NX] for c in range(chans)])
            sf[0, 1, z, :NX] = packed([gs[0, z + 1, c, :NX] for c in range(chans)])

        over_z(pack_fields)
        pl.semaphore_wait(barrier, len(greeted))
        send(row_copies(0, lambda r: hs.at[0, inside, pl.ds(0, chans), r]))
        send(row_copies(1, lambda r: gs.at[0, inside, pl.ds(0, chans), r]))
        send(strip_copies(0, lambda column, r: sf.at[column, pl.ds(0, 2), pl.ds(0, zs), r]))

        biases = [bias_ref[k] for k in range(6)]
        for load in feats_in:
            load.wait()

        def head(z):
            logits = jnp.dot(wide[...], feat[z], preferred_element_type=F32)
            active = [jax.nn.sigmoid(logits[k * NX : (k + 1) * NX] + biases[k]) for k in range(6)]
            summed = active[0]
            for k in range(1, 6):
                summed = summed + active[k]
            inverse = 1.0 / (summed + 1.0)
            coupling = [active[k] * inverse for k in range(6)]
            for k in range(6):
                act[z, k] = active[k]
                kap[z + 1, k, :NX] = coupling[k]
            inv[z] = inverse
            sk[0, z, :NX] = packed(coupling)

        over_z(head)
        send(row_copies(2, lambda r: kap.at[inside, pl.ds(0, 6), r]))
        send(strip_copies(1, lambda column, r: sk.at[column, pl.ds(0, zs), r]))
        for copy in arriving:
            copy.wait_recv()

        def clear(rows):
            hs[0, 1 : zs + 1, :chans, rows] = jnp.zeros((zs, chans, 4, NY), F32)
            kap[1 : zs + 1, :6, rows] = jnp.zeros((zs, 6, 4, NY), F32)

        @pl.when(me_x == gx - 1)
        def _():
            clear(slice(NX, NX + 4))

        @pl.when(me_x == 0)
        def _():
            clear(slice(NX + 4, RING))

        def assemble(z):
            hs[0, z + 1, chans] = unpacked(sf[0, 0, z], sf[1, 0, z], sf[2, 0, z])
            gs[0, z + 1, chans] = unpacked(sf[0, 1, z], sf[1, 1, z], sf[2, 1, z])
            flat[pl.ds(z * RING, RING)] = unpacked(sk[0, z], sk[1, z], sk[2, z])

        over_z(assemble)
        strips = jnp.dot(
            flat[...], expand[...], precision=lax.Precision.HIGHEST, preferred_element_type=F32
        )
        for z in range(zs):
            for coefs, value in (
                (kst, [strips[z * RING : (z + 1) * RING, k * NY : (k + 1) * NY] for k in range(6)]),
                (kap, [kap[z + 1, k] for k in range(6)]),
            ):
                centre = 1.0
                for k in range(6):
                    centre = centre - value[k]
                    if coefs is kst:
                        coefs[z + 1, k] = value[k]
                coefs[z + 1, 6] = centre

        def columns(strip, j):
            return jnp.stack(
                [
                    jnp.broadcast_to(strip[:, c * EDGE + j : c * EDGE + j + 1], strip.shape)
                    for c in range(chans)
                ]
            )

        def around(rnd, z, rows):
            h, strip = hs[rnd, z + 1, :chans], hs[rnd, z + 1, chans, :rows]
            shape = (chans, rows, NY)
            lanes = iota(shape, 2)
            centre = h[:, :rows]
            return centre, [
                pltpu.roll(h, RING - 1, 1)[:, :rows],
                pltpu.roll(h, 1, 1)[:, :rows],
                jnp.where(lanes == NY - 1, columns(strip, HIGH), pltpu.roll(centre, NY - 1, 2)),
                jnp.where(lanes == 0, columns(strip, LOW), pltpu.roll(centre, 1, 2)),
                hs[rnd, z + 2, :chans, :rows],
                hs[rnd, z, :chans, :rows],
            ]

        def forward(rnd, z):
            h, beside = around(rnd, z, RING)
            result = kap[z + 1, 6] * h
            for k in range(6):
                result = result + kap[z + 1, k] * beside[k]
            strip = hs[rnd, z + 1, chans]
            edge = kst[z + 1, 6] * strip
            for k, value in enumerate((
                pltpu.roll(strip, RING - 1, 0),
                pltpu.roll(strip, 1, 0),
                pltpu.roll(strip, NY - 1, 1),
                pltpu.roll(strip, 1, 1),
                hs[rnd, z + 2, chans],
                hs[rnd, z, chans],
            )):
                edge = edge + kst[z + 1, k] * value
            hs[rnd + 1, z + 1, :chans] = result
            hs[rnd + 1, z + 1, chans] = edge

        def backward(rnd, z, rows):
            g, strip = gs[rnd, z + 1, :chans], gs[rnd, z + 1, chans]
            lanes = iota((chans, rows, NY), 2)
            near = g[:, :rows]
            edge = [kst[z + 1, k] * strip for k in range(4)]
            result = kap[z + 1, 6, :rows] * near
            result = result + pltpu.roll(kap[z + 1, 0] * g, 1, 1)[:, :rows]
            result = result + pltpu.roll(kap[z + 1, 1] * g, RING - 1, 1)[:, :rows]
            result = result + jnp.where(
                lanes == 0,
                columns(edge[2][:rows], LOW),
                pltpu.roll(kap[z + 1, 2, :rows] * near, 1, 2),
            )
            result = result + jnp.where(
                lanes == NY - 1,
                columns(edge[3][:rows], HIGH),
                pltpu.roll(kap[z + 1, 3, :rows] * near, NY - 1, 2),
            )
            result = result + kap[z, 4, :rows] * gs[rnd, z, :chans, :rows]
            result = result + kap[z + 2, 5, :rows] * gs[rnd, z + 2, :chans, :rows]
            if rows == NX:
                return result
            strip = kst[z + 1, 6] * strip
            strip = strip + pltpu.roll(edge[0], 1, 0) + pltpu.roll(edge[1], RING - 1, 0)
            strip = strip + pltpu.roll(edge[2], 1, 1) + pltpu.roll(edge[3], NY - 1, 1)
            strip = strip + kst[z, 4] * gs[rnd, z, chans] + kst[z + 2, 5] * gs[rnd, z + 2, chans]
            gs[rnd + 1, z + 1, :chans] = result
            gs[rnd + 1, z + 1, chans] = strip

        for rnd in range(ITERS - 1):

            def advance(z, rnd=rnd):
                forward(rnd, z)
                backward(rnd, z, RING)

            over_z(advance)

        bias_acc[...] = jnp.zeros((6, NX, NY), F32)

        def slopes(z):
            parts = [jnp.zeros((NX, NY), F32) for _ in range(7)]
            for rnd in range(ITERS):
                g = gs[ITERS - 1 - rnd, z + 1, :chans, :NX]
                h, beside = around(rnd, z, NX)
                for k in range(6):
                    parts[k] = parts[k] + jnp.sum(g * beside[k], 0)
                parts[6] = parts[6] + jnp.sum(g * h, 0)
            inner_sum = jnp.zeros((NX, NY), F32)
            effective = []
            for k in range(6):
                value = parts[k] - parts[6]
                effective.append(value)
                inner_sum = inner_sum + value * kap[z + 1, k, :NX]
            pieces = []
            for k in range(6):
                active = act[z, k]
                slope = (effective[k] - inner_sum) * inv[z] * active * (1.0 - active)
                bias_acc[k] += slope
                pieces.append(slope)
            dlow[z] = jnp.concatenate(pieces, axis=0).astype(BF16)

        over_z(slopes)

        total = jnp.zeros((6 * NX, feats * NX), F32)
        for z in range(0, zs, 2):
            total = total + lax.dot_general(
                jnp.concatenate([dlow[z], dlow[z + 1]], axis=1),
                jnp.concatenate([feat[z], feat[z + 1]], axis=1),
                (((1,), (1,)), ((), ())),
                preferred_element_type=F32,
            )
        total = jnp.where(same_x, total, 0.0)
        by_k = jnp.concatenate(
            [jnp.sum(total[k * NX : (k + 1) * NX], 0, keepdims=True) for k in range(6)]
            + [jnp.zeros((2, feats * NX), F32)],
            axis=0,
        )
        fold = ((iota((feats * NX, 2 * feats), 0) >> 3) == iota((feats * NX, 2 * feats), 1)).astype(F32)
        by_f = jnp.dot(by_k, fold, precision=lax.Precision.HIGHEST, preferred_element_type=F32)
        lane_row = iota((1, NY), 1)
        payload = [
            jnp.where(
                lane_row < feats,
                by_f[2 * r : 2 * r + 1],
                pltpu.roll(by_f[2 * r + 1 : 2 * r + 2], feats, 1),
            )
            for r in range(3)
        ]
        bias_row = jnp.zeros((1, NY), F32)
        for k in range(6):
            amount = jnp.sum(jnp.sum(bias_acc[k], 0, keepdims=True), 1, keepdims=True)
            bias_row = jnp.where(lane_row == k, amount, bias_row)
        payload = jnp.concatenate(payload + [bias_row], axis=0)

        def exchange(buffer, me, partners, send_sem, recv_sem, value):
            buffer[me] = value
            copies = [
                remote(buffer.at[me], buffer.at[me], send_sem.at[d], recv_sem.at[d], partner)
                for d, partner in enumerate(partners)
            ]
            for copy in copies:
                copy.start()
            pending.extend(copies)
            return copies

        def gather(buffer, copies, count):
            for copy in copies:
                copy.wait_recv()
            value = buffer[0]
            for i in range(1, count):
                value = value + buffer[i]
            return value

        first = exchange(sum_a, me_y, partners_a, sa_sem, ra_sem, payload)

        def finish(z):
            g_out[z] = backward(ITERS - 1, z, NX)

        over_z(finish)
        store = pltpu.make_async_copy(g_out, out_hbm, local_sem.at[2 + zs])
        store.start()

        value = gather(sum_a, first, gy)
        second = exchange(sum_b, me_in, partners_b, sb_sem, rb_sem, value)
        value = gather(sum_b, second, inner)
        third = exchange(sum_c, me_out, partners_c, sc_sem, rc_sem, value)
        sum_ref[...] = gather(sum_c, third, outer) * factor
        for copy in pending:
            copy.wait_send()
        store.wait()

    return kernel


def deliver(feats):
    def kernel(field, sums, grad_probs, grad_weight, grad_bias, sems):
        copies = [
            pltpu.make_async_copy(field.at[z], grad_probs.at[z], sems.at[z])
            for z in range(field.shape[0])
        ]
        for copy in copies:
            copy.start()
        for k in range(6):
            row = sums[k // 2 : k // 2 + 1, :]
            if k % 2:
                row = pltpu.roll(row, feats, 1)
            grad_weight[k : k + 1, :] = row[:, :feats]
        grad_bias[...] = sums[3:4, :6]
        for copy in copies:
            copy.wait()

    return kernel


def inner_of(gx):
    return 8 if gx == 64 else 2


def per_device(features, head_weight, head_bias, probs, cotangent):
    zs, feats, nx, ny = features.shape
    chans = probs.shape[1]
    gx, gy = lax.axis_size("gx"), lax.axis_size("gy")
    inner = inner_of(gx)
    outer = gx // inner
    factor = 1.0 / math.sqrt(zs * nx * ny * gx * gy)
    dma = pltpu.SemaphoreType.DMA
    hbm = pl.BlockSpec(memory_space=pltpu.HBM)
    vmem = pl.BlockSpec(memory_space=pltpu.VMEM)
    field = pltpu.VMEM((ITERS, zs + 2, chans + 1, RING, ny), F32)
    coefs = pltpu.VMEM((zs + 2, 7, RING, ny), F32)
    grad_field, sums = pl.pallas_call(
        make_kernel(zs, chans, feats, gx, gy, inner, factor),
        out_shape=(
            jax.ShapeDtypeStruct(probs.shape, F32),
            jax.ShapeDtypeStruct((4, ny), F32),
        ),
        in_specs=[hbm, vmem, pl.BlockSpec(memory_space=pltpu.SMEM), hbm, hbm],
        out_specs=(hbm, vmem),
        scratch_shapes=[
            pltpu.VMEM((zs, feats * nx, ny), BF16),
            field,
            field,
            pltpu.VMEM((zs, chans, nx, ny), F32),
            coefs,
            coefs,
            pltpu.VMEM((zs, 6, nx, ny), F32),
            pltpu.VMEM((zs, nx, ny), F32),
            pltpu.VMEM((zs, 6 * nx, ny), BF16),
            pltpu.VMEM((6, nx, ny), F32),
            pltpu.VMEM((6 * nx, feats * nx), BF16),
            pltpu.VMEM((ny, 6 * ny), F32),
            pltpu.VMEM((3, 2, zs, RING, ny), F32),
            pltpu.VMEM((3, zs, RING, ny), F32),
            pltpu.VMEM((zs * RING, ny), F32),
            pltpu.VMEM((gy, 4, ny), F32),
            pltpu.VMEM((inner, 4, ny), F32),
            pltpu.VMEM((outer, 4, ny), F32),
            dma((3 + zs,)),
            dma((3, 2)),
            dma((3, 2)),
            dma((2, len(SIDES))),
            dma((2, len(SIDES))),
            dma((gy - 1,)),
            dma((gy - 1,)),
            dma((inner - 1,)),
            dma((inner - 1,)),
            dma((outer - 1,)),
            dma((outer - 1,)),
        ],
        compiler_params=pltpu.CompilerParams(
            collective_id=0, has_side_effects=True, vmem_limit_bytes=63 * 1024 * 1024
        ),
        name="spread_backward",
    )(features.reshape(zs, feats * nx, ny), head_weight, head_bias, probs, cotangent)
    grad_probs, grad_weight, grad_bias = pl.pallas_call(
        deliver(feats),
        out_shape=(
            jax.ShapeDtypeStruct(probs.shape, F32),
            jax.ShapeDtypeStruct((6, feats), F32),
            jax.ShapeDtypeStruct((1, 6), F32),
        ),
        in_specs=[pl.BlockSpec(memory_space=pl.ANY), vmem],
        out_specs=(hbm, vmem, vmem),
        scratch_shapes=[dma((zs,))],
        name="deliver",
    )(grad_field, sums)
    return grad_probs, grad_weight, grad_bias.reshape(6)


def solution(mesh):
    spec = P(None, None, "gx", "gy")
    return jax.shard_map(
        per_device,
        mesh=mesh,
        in_specs=(spec, P(), P(), spec, spec),
        out_specs=(spec, P(), P()),
        check_vma=False,
    )
```

time: 60.7 us -> 66 us (1.087)
  Pallas kernels: 57 us -> 65.1 us
  local copies, waits for them, and re-layouts: 2.86 us -> 0 us
    pallas_call x0 -> x1, Pallas kernels: none -> 10.4 us  [per_device(): pl.pallas_call(deliver(feats), out_shape=(jax.ShapeDtypeStruct(probs.shap...]
    unnamed x7 -> x0, local copies, waits for them, and re-layouts: 2.86 us -> none
    pallas_call x1, Pallas kernels: 57 us -> 54.7 us  [per_device(): pl.pallas_call(make_kernel(zs, chans, feats, gx, gy, inner, factor), out_...]
where the time goes in v2:
time: 66 us; the launch traced here: 65.8 us
  Pallas kernels  65.1 us (99%)
    pallas_call x1, Pallas kernels, per_device(): pl.pallas_call(make_kernel(zs, chans, feats, gx, gy, inner, factor), out_...  54.7 us
    pallas_call x1, Pallas kernels, per_device(): pl.pallas_call(deliver(feats), out_shape=(jax.ShapeDtypeStruct(probs.shap...  10.4 us

profile of v2, /device:TPU:1, one launch (start us, length us, event | category | flops | bytes accessed | tf_op | source)
XLA Modules:
  0.0 65.8 jit_solution(16224178366598642693)
XLA Ops:
  0.6 54.7 %spread_backward.1 = (f32[8,8,8,128]{3,2,1,0:T(8,128)}, f32[4,128]{1,0:T(4,128)}) custom-call(bf16[8,512,128]{2,1,0:T(8,128)(2,1)} %bitcast.2, bf16[6,64]{1,0:T(8,128)(2,1)} %weight_ref.1, f32[6]{0:T(128)} %bias_ref.1, f32[8,8,8,128]{3,2,1,0:T(8,128)} %probs_hbm.1, f32[8,8,8,128]{3,2,1,0:T(8,128)} %cot_hbm.1), custom_call_target="tpu_custom_call" | custom-call | tf_op jit(solution)/shard_map/spread_backward/pallas_call | solution.py:434
  55.4 10.4 %deliver.1 = (f32[8,8,8,128]{3,2,1,0:T(8,128)}, f32[6,64]{1,0:T(8,128)}, f32[1,6]{1,0:T(1,128)}) custom-call(f32[8,8,8,128]{3,2,1,0:T(8,128)} %get-tuple-element.8.field, f32[4,128]{1,0:T(4,128)} %get-tuple-element.9.sums), custom_call_target="tpu_custom_call" | custom-call | tf_op jit(solution)/shard_map/deliver/pallas_call | solution.py:478

commit v3 on v2

--- a/solution.py
+++ b/solution.py
@@ -22,12 +22,12 @@
     return lax.broadcasted_iota(jnp.int32, shape, dim)
 
 
-def rows_of(dx):
+def rows_of(dx, count):
     if dx == 0:
         return pl.ds(0, NX), pl.ds(0, NX)
     if dx > 0:
-        return pl.ds(NX - 3, 3), pl.ds(RING - 3, 3)
-    return pl.ds(0, 3), pl.ds(NX, 3)
+        return pl.ds(NX - count, count), pl.ds(RING - count, count)
+    return pl.ds(0, count), pl.ds(NX, count)
 
 
 def make_kernel(zs, chans, feats, gx, gy, inner, factor):
@@ -38,7 +38,7 @@
         feat_hbm, weight_ref, bias_ref, probs_hbm, cot_hbm,
         out_hbm, sum_ref,
         feat, hs, gs, g_out, kap, kst, act, inv, dlow, bias_acc, wide, expand,
-        sf, sk, flat, sum_a, sum_b, sum_c,
+        sf, sk, flat, far_g, far_k, sum_a, sum_b, sum_c,
         local_sem, row_send, row_recv, strip_send, strip_recv,
         sa_sem, ra_sem, sb_sem, rb_sem, sc_sem, rc_sem,
     ):
@@ -52,10 +52,6 @@
         partners_b = [(me_out * inner + lax.rem(me_in + d, inner), me_y) for d in range(1, inner)]
         partners_c = [(lax.rem(me_out + d, outer) * inner + me_in, me_y) for d in range(1, outer)]
         greeted = [at(dx, dy) for dx, dy in SIDES if dx] + partners_a + partners_b + partners_c
-        barrier = pltpu.get_barrier_semaphore()
-        for partner in greeted:
-            pl.semaphore_signal(barrier, inc=1, device_id=partner, device_id_type=MESH)
-
         fields_in = [
             pltpu.make_async_copy(source, field.at[0, inside, pl.ds(0, chans), pl.ds(0, NX)], local_sem.at[i])
             for i, (source, field) in enumerate(((probs_hbm, hs), (cot_hbm, gs)))
@@ -63,7 +59,12 @@
         feats_in = [
             pltpu.make_async_copy(feat_hbm.at[z], feat.at[z], local_sem.at[2 + z]) for z in range(zs)
         ]
-        for load in fields_in + feats_in:
+        for load in fields_in:
+            load.start()
+        barrier = pltpu.get_barrier_semaphore()
+        for partner in greeted:
+            pl.semaphore_signal(barrier, inc=1, device_id=partner, device_id_type=MESH)
+        for load in feats_in:
             load.start()
 
         for field in (hs, gs):
@@ -101,14 +102,18 @@
                 tile = jnp.where((lane >> 4) == i, pltpu.roll(value, i * EDGE + 4, 1), tile)
             return jnp.where(lane_j < 8, tile, 0.0)
 
-        def unpacked(own, low, high):
+        def unpacked(own, low, high, first):
             seen = (
                 (ring_row < NX) | ((ring_row < NX + 4) & has_right) | ((ring_row >= NX + 4) & has_left)
             )
             low = jnp.where(has_down, low, 0.0)
             high = jnp.where(has_up, high, 0.0)
-            near = jnp.where(ring_j < 4, low, own)
-            far = pltpu.roll(jnp.where(ring_j < 4, own, high), 8, 1)
+            near = jnp.where(ring_j < first + 4, low, own)
+            far = jnp.where(ring_j < first + 4, own, high)
+            if first:
+                near = pltpu.roll(near, NY - first, 1)
+            else:
+                far = pltpu.roll(far, 8, 1)
             return jnp.where(seen, jnp.where(ring_j < 8, near, far), 0.0)
 
         def over_z(body):
@@ -126,25 +131,37 @@
 
         pending, arriving = [], []
 
-        def send(copies):
+        def send(copies, awaited=True):
             for copy in copies:
                 copy.start()
             pending.extend(copies)
-            arriving.extend(copies)
-
-        def row_copies(which, view):
+            if awaited:
+                arriving.extend(copies)
+            return copies
+
+        def row_copies(which, count, view):
             return [
                 remote(
-                    view(rows_of(dx)[0]), view(rows_of(dx)[1]),
+                    view(rows_of(dx, count)[0]), view(rows_of(dx, count)[1]),
                     row_send.at[which, i], row_recv.at[which, i], at(dx, 0),
                 )
                 for i, dx in enumerate((1, -1))
             ]
 
-        def strip_copies(which, view):
+        def far_copies(which, view, target):
             return [
                 remote(
-                    view(0, rows_of(dx)[0]), view((0, 1, 2)[dy], rows_of(dx)[1]),
+                    view(pl.ds(row, 1)), target.at[i, pl.ds(0, zs), pl.ds(0, target.shape[2]), pl.ds(0, 1)],
+                    row_send.at[which, i], row_recv.at[which, i], at(dx, 0),
+                )
+                for i, (dx, row) in enumerate(((1, NX - 3), (-1, 2)))
+            ]
+
+        def strip_copies(which, strip):
+            return [
+                remote(
+                    strip.at[0, pl.ds(0, zs), rows_of(dx, 3)[0]],
+                    strip.at[(0, 1, 2)[dy], pl.ds(0, zs), rows_of(dx, 3)[1]],
                     strip_send.at[which, i], strip_recv.at[which, i], at(dx, dy),
                 )
                 for i, (dx, dy) in enumerate(SIDES)
@@ -154,14 +171,17 @@
             load.wait()
 
         def pack_fields(z):
-            sf[0, 0, z, :NX] = packed([hs[0, z + 1, c, :NX] for c in range(chans)])
-            sf[0, 1, z, :NX] = packed([gs[0, z + 1, c, :NX] for c in range(chans)])
+            of_h = packed([hs[0, z + 1, c, :NX] for c in range(chans)])
+            of_g = packed([gs[0, z + 1, c, :NX] for c in range(chans)])
+            sf[0, z, :NX] = of_h + pltpu.roll(of_g, 8, 1)
 
         over_z(pack_fields)
         pl.semaphore_wait(barrier, len(greeted))
-        send(row_copies(0, lambda r: hs.at[0, inside, pl.ds(0, chans), r]))
-        send(row_copies(1, lambda r: gs.at[0, inside, pl.ds(0, chans), r]))
-        send(strip_copies(0, lambda column, r: sf.at[column, pl.ds(0, 2), pl.ds(0, zs), r]))
+        g_rows = lambda r: gs.at[0, inside, pl.ds(0, chans), r]
+        k_rows = lambda r: kap.at[inside, pl.ds(0, 6), r]
+        send(row_copies(0, 3, lambda r: hs.at[0, inside, pl.ds(0, chans), r]))
+        send(row_copies(1, 2, g_rows))
+        send(strip_copies(0, sf))
 
         biases = [bias_ref[k] for k in range(6)]
         for load in feats_in:
@@ -182,8 +202,9 @@
             sk[0, z, :NX] = packed(coupling)
 
         over_z(head)
-        send(row_copies(2, lambda r: kap.at[inside, pl.ds(0, 6), r]))
-        send(strip_copies(1, lambda column, r: sk.at[column, pl.ds(0, zs), r]))
+        send(row_copies(2, 2, k_rows))
+        send(strip_copies(1, sk))
+        outermost = send(far_copies(3, g_rows, far_g) + far_copies(4, k_rows, far_k), awaited=False)
         for copy in arriving:
             copy.wait_recv()
 
@@ -200,9 +221,9 @@
             clear(slice(NX + 4, RING))
 
         def assemble(z):
-            hs[0, z + 1, chans] = unpacked(sf[0, 0, z], sf[1, 0, z], sf[2, 0, z])
-            gs[0, z + 1, chans] = unpacked(sf[0, 1, z], sf[1, 1, z], sf[2, 1, z])
-            flat[pl.ds(z * RING, RING)] = unpacked(sk[0, z], sk[1, z], sk[2, z])
+            hs[0, z + 1, chans] = unpacked(sf[0, z], sf[1, z], sf[2, z], 0)
+            gs[0, z + 1, chans] = unpacked(sf[0, z], sf[1, z], sf[2, z], 8)
+            flat[pl.ds(z * RING, RING)] = unpacked(sk[0, z], sk[1, z], sk[2, z], 0)
 
         over_z(assemble)
         strips = jnp.dot(
@@ -324,22 +345,23 @@
 
         over_z(slopes)
 
-        total = jnp.zeros((6 * NX, feats * NX), F32)
+        cells = feats * NX
+        total = jnp.zeros((cells, 6 * NX), F32)
         for z in range(0, zs, 2):
             total = total + lax.dot_general(
+                jnp.concatenate([feat[z], feat[z + 1]], axis=1),
                 jnp.concatenate([dlow[z], dlow[z + 1]], axis=1),
-                jnp.concatenate([feat[z], feat[z + 1]], axis=1),
                 (((1,), (1,)), ((), ())),
                 preferred_element_type=F32,
             )
-        total = jnp.where(same_x, total, 0.0)
-        by_k = jnp.concatenate(
-            [jnp.sum(total[k * NX : (k + 1) * NX], 0, keepdims=True) for k in range(6)]
-            + [jnp.zeros((2, feats * NX), F32)],
-            axis=0,
+        total = jnp.where((iota((cells, 6 * NX), 0) & 7) == (iota((cells, 6 * NX), 1) & 7), total, 0.0)
+        over_f = ((iota((2 * feats, cells), 1) >> 3) == iota((2 * feats, cells), 0)).astype(F32)
+        over_k = ((iota((8, 6 * NX), 1) >> 3) == iota((8, 6 * NX), 0)).astype(F32)
+        by_f = jnp.dot(over_f, total, precision=lax.Precision.HIGHEST, preferred_element_type=F32)
+        by_f = lax.dot_general(
+            over_k, by_f, (((1,), (1,)), ((), ())),
+            precision=lax.Precision.HIGHEST, preferred_element_type=F32,
         )
-        fold = ((iota((feats * NX, 2 * feats), 0) >> 3) == iota((feats * NX, 2 * feats), 1)).astype(F32)
-        by_f = jnp.dot(by_k, fold, precision=lax.Precision.HIGHEST, preferred_element_type=F32)
         lane_row = iota((1, NY), 1)
         payload = [
             jnp.where(
@@ -376,6 +398,22 @@
 
         first = exchange(sum_a, me_y, partners_a, sa_sem, ra_sem, payload)
 
+        for copy in outermost:
+            copy.wait_recv()
+
+        def widen(z):
+            for i, (known, row) in enumerate(((has_left, RING - 3), (has_right, NX + 2))):
+                gs[0, z + 1, :chans, row : row + 1] = far_g[i, z, :, :1]
+                kap[z + 1, :6, row : row + 1] = jnp.where(known, far_k[i, z, :, :1], 0.0)
+            centre = 1.0
+            for k in range(6):
+                centre = centre - kap[z + 1, k, NX:]
+            kap[z + 1, 6, NX:] = centre
+
+        over_z(widen)
+        for rnd in range(ITERS - 1):
+            over_z(lambda z, rnd=rnd: backward(rnd, z, RING))
+
         def finish(z):
             g_out[z] = backward(ITERS - 1, z, NX)
 
@@ -396,21 +434,23 @@
 
 
 def deliver(feats):
-    def kernel(field, sums, grad_probs, grad_weight, grad_bias, sems):
-        copies = [
-            pltpu.make_async_copy(field.at[z], grad_probs.at[z], sems.at[z])
-            for z in range(field.shape[0])
-        ]
-        for copy in copies:
-            copy.start()
+    def kernel(field, sums, grad_probs, grad_weight, grad_bias, held, sems):
+        planes = range(field.shape[0])
+        loads = [pltpu.make_async_copy(field.at[z], held.at[z], sems.at[0, z]) for z in planes]
+        stores = [pltpu.make_async_copy(held.at[z], grad_probs.at[z], sems.at[1, z]) for z in planes]
+        for load in loads:
+            load.start()
         for k in range(6):
             row = sums[k // 2 : k // 2 + 1, :]
             if k % 2:
                 row = pltpu.roll(row, feats, 1)
             grad_weight[k : k + 1, :] = row[:, :feats]
         grad_bias[...] = sums[3:4, :6]
-        for copy in copies:
-            copy.wait()
+        for load, store in zip(loads, stores):
+            load.wait()
+            store.start()
+        for store in stores:
+            store.wait()
 
     return kernel
 
@@ -452,15 +492,17 @@
             pltpu.VMEM((6, nx, ny), F32),
             pltpu.VMEM((6 * nx, feats * nx), BF16),
             pltpu.VMEM((ny, 6 * ny), F32),
-            pltpu.VMEM((3, 2, zs, RING, ny), F32),
+            pltpu.VMEM((3, zs, RING, ny), F32),
             pltpu.VMEM((3, zs, RING, ny), F32),
             pltpu.VMEM((zs * RING, ny), F32),
+            pltpu.VMEM((2, zs, chans, nx, ny), F32),
+            pltpu.VMEM((2, zs, 6, nx, ny), F32),
             pltpu.VMEM((gy, 4, ny), F32),
             pltpu.VMEM((inner, 4, ny), F32),
             pltpu.VMEM((outer, 4, ny), F32),
             dma((3 + zs,)),
-            dma((3, 2)),
-            dma((3, 2)),
+            dma((5, 2)),
+            dma((5, 2)),
             dma((2, len(SIDES))),
             dma((2, len(SIDES))),
             dma((gy - 1,)),
@@ -482,9 +524,9 @@
             jax.ShapeDtypeStruct((6, feats), F32),
             jax.ShapeDtypeStruct((1, 6), F32),
         ),
-        in_specs=[pl.BlockSpec(memory_space=pl.ANY), vmem],
+        in_specs=[hbm, vmem],
         out_specs=(hbm, vmem, vmem),
-        scratch_shapes=[dma((zs,))],
+        scratch_shapes=[pltpu.VMEM(probs.shape, F32), dma((2, zs))],
         name="deliver",
     )(grad_field, sums)
     return grad_probs, grad_weight, grad_bias.reshape(6)

time: 66 us -> 57.7 us (0.87)
  Pallas kernels: 65.1 us -> 56.8 us
    pallas_call x1, Pallas kernels: 10.4 us -> 2.9 us  [per_device(): pl.pallas_call(deliver(feats), out_shape=(jax.ShapeDtypeStruct(probs.shap...]
    pallas_call x1, Pallas kernels: 54.7 us -> 53.9 us  [per_device(): pl.pallas_call(make_kernel(zs, chans, feats, gx, gy, inner, factor), out_...]
where the time goes in v3:
time: 57.7 us; the launch traced here: 57.4 us
  Pallas kernels  56.8 us (98%)
  between operations  0.64 us (1%)
    pallas_call x1, Pallas kernels, per_device(): pl.pallas_call(make_kernel(zs, chans, feats, gx, gy, inner, factor), out_...  53.9 us
    pallas_call x1, Pallas kernels, per_device(): pl.pallas_call(deliver(feats), out_shape=(jax.ShapeDtypeStruct(probs.shap...  2.9 us

profile of v3, /device:TPU:1, one launch (start us, length us, event | category | flops | bytes accessed | tf_op | source)
XLA Modules:
  0.0 57.4 jit_solution(10684860440052808235)
XLA Ops:
  0.6 53.9 %spread_backward.1 = (f32[8,8,8,128]{3,2,1,0:T(8,128)}, f32[4,128]{1,0:T(4,128)}) custom-call(bf16[8,512,128]{2,1,0:T(8,128)(2,1)} %bitcast.2, bf16[6,64]{1,0:T(8,128)(2,1)} %weight_ref.1, f32[6]{0:T(128)} %bias_ref.1, f32[8,8,8,128]{3,2,1,0:T(8,128)} %probs_hbm.1, f32[8,8,8,128]{3,2,1,0:T(8,128)} %cot_hbm.1), custom_call_target="tpu_custom_call" | custom-call | tf_op jit(solution)/shard_map/spread_backward/pallas_call | solution.py:474
  54.5 2.9 %deliver.1 = (f32[8,8,8,128]{3,2,1,0:T(8,128)}, f32[6,64]{1,0:T(8,128)}, f32[1,6]{1,0:T(1,128)}) custom-call(f32[8,8,8,128]{3,2,1,0:T(8,128)} %get-tuple-element.8.field, f32[4,128]{1,0:T(4,128)} %get-tuple-element.9.sums), custom_call_target="tpu_custom_call" | custom-call | tf_op jit(solution)/shard_map/deliver/pallas_call | solution.py:520

commit v4 on v3

--- a/solution.py
+++ b/solution.py
@@ -139,10 +139,10 @@
                 arriving.extend(copies)
             return copies
 
-        def row_copies(which, count, view):
+        def row_copies(which, count, source, target):
             return [
                 remote(
-                    view(rows_of(dx, count)[0]), view(rows_of(dx, count)[1]),
+                    source(rows_of(dx, count)[0]), target(rows_of(dx, count)[1]),
                     row_send.at[which, i], row_recv.at[which, i], at(dx, 0),
                 )
                 for i, dx in enumerate((1, -1))
@@ -167,6 +167,10 @@
                 for i, (dx, dy) in enumerate(SIDES)
             ]
 
+        pl.semaphore_wait(barrier, len(greeted))
+        planes, every = pl.ds(0, zs), pl.ds(0, chans)
+        send(row_copies(0, 3, lambda r: probs_hbm.at[planes, every, r], lambda r: hs.at[0, inside, every, r]))
+        send(row_copies(1, 2, lambda r: cot_hbm.at[planes, every, r], lambda r: gs.at[0, inside, every, r]))
         for load in fields_in:
             load.wait()
 
@@ -176,11 +180,6 @@
             sf[0, z, :NX] = of_h + pltpu.roll(of_g, 8, 1)
 
         over_z(pack_fields)
-        pl.semaphore_wait(barrier, len(greeted))
-        g_rows = lambda r: gs.at[0, inside, pl.ds(0, chans), r]
-        k_rows = lambda r: kap.at[inside, pl.ds(0, 6), r]
-        send(row_copies(0, 3, lambda r: hs.at[0, inside, pl.ds(0, chans), r]))
-        send(row_copies(1, 2, g_rows))
         send(strip_copies(0, sf))
 
         biases = [bias_ref[k] for k in range(6)]
@@ -202,9 +201,14 @@
             sk[0, z, :NX] = packed(coupling)
 
         over_z(head)
-        send(row_copies(2, 2, k_rows))
+        k_rows = lambda r: kap.at[inside, pl.ds(0, 6), r]
+        send(row_copies(2, 2, k_rows, k_rows))
         send(strip_copies(1, sk))
-        outermost = send(far_copies(3, g_rows, far_g) + far_copies(4, k_rows, far_k), awaited=False)
+        outermost = send(
+            far_copies(3, lambda r: cot_hbm.at[planes, every, r], far_g)
+            + far_copies(4, k_rows, far_k),
+            awaited=False,
+        )
         for copy in arriving:
             copy.wait_recv()
 
@@ -396,7 +400,7 @@
                 value = value + buffer[i]
             return value
 
-        first = exchange(sum_a, me_y, partners_a, sa_sem, ra_sem, payload)
+        first = exchange(sum_c, me_out, partners_c, sc_sem, rc_sem, payload)
 
         for copy in outermost:
             copy.wait_recv()
@@ -411,8 +415,10 @@
             kap[z + 1, 6, NX:] = centre
 
         over_z(widen)
-        for rnd in range(ITERS - 1):
-            over_z(lambda z, rnd=rnd: backward(rnd, z, RING))
+        over_z(lambda z: backward(0, z, RING))
+        value = gather(sum_c, first, outer)
+        second = exchange(sum_a, me_y, partners_a, sa_sem, ra_sem, value)
+        over_z(lambda z: backward(1, z, RING))
 
         def finish(z):
             g_out[z] = backward(ITERS - 1, z, NX)
@@ -420,12 +426,9 @@
         over_z(finish)
         store = pltpu.make_async_copy(g_out, out_hbm, local_sem.at[2 + zs])
         store.start()
-
-        value = gather(sum_a, first, gy)
-        second = exchange(sum_b, me_in, partners_b, sb_sem, rb_sem, value)
-        value = gather(sum_b, second, inner)
-        third = exchange(sum_c, me_out, partners_c, sc_sem, rc_sem, value)
-        sum_ref[...] = gather(sum_c, third, outer) * factor
+        value = gather(sum_a, second, gy)
+        third = exchange(sum_b, me_in, partners_b, sb_sem, rb_sem, value)
+        sum_ref[...] = gather(sum_b, third, inner) * factor
         for copy in pending:
             copy.wait_send()
         store.wait()
@@ -434,23 +437,32 @@
 
 
 def deliver(feats):
-    def kernel(field, sums, grad_probs, grad_weight, grad_bias, held, sems):
+    def kernel(field, sums, grad_probs, grad_weight, grad_bias, held, sums_in, weight_out, bias_out, sems, small):
         planes = range(field.shape[0])
         loads = [pltpu.make_async_copy(field.at[z], held.at[z], sems.at[0, z]) for z in planes]
         stores = [pltpu.make_async_copy(held.at[z], grad_probs.at[z], sems.at[1, z]) for z in planes]
+        first = pltpu.make_async_copy(sums, sums_in, small.at[0])
+        last = [
+            pltpu.make_async_copy(weight_out, grad_weight, small.at[1]),
+            pltpu.make_async_copy(bias_out, grad_bias, small.at[2]),
+        ]
+        first.start()
         for load in loads:
             load.start()
+        first.wait()
         for k in range(6):
-            row = sums[k // 2 : k // 2 + 1, :]
+            row = sums_in[k // 2 : k // 2 + 1, :]
             if k % 2:
                 row = pltpu.roll(row, feats, 1)
-            grad_weight[k : k + 1, :] = row[:, :feats]
-        grad_bias[...] = sums[3:4, :6]
+            weight_out[k : k + 1, :] = row[:, :feats]
+        bias_out[...] = sums_in[3:4, :6]
+        for copy in last:
+            copy.start()
         for load, store in zip(loads, stores):
             load.wait()
             store.start()
-        for store in stores:
-            store.wait()
+        for copy in stores + last:
+            copy.wait()
 
     return kernel
 
@@ -524,9 +536,16 @@
             jax.ShapeDtypeStruct((6, feats), F32),
             jax.ShapeDtypeStruct((1, 6), F32),
         ),
-        in_specs=[hbm, vmem],
-        out_specs=(hbm, vmem, vmem),
-        scratch_shapes=[pltpu.VMEM(probs.shape, F32), dma((2, zs))],
+        in_specs=[hbm, hbm],
+        out_specs=(hbm, hbm, hbm),
+        scratch_shapes=[
+            pltpu.VMEM(probs.shape, F32),
+            pltpu.VMEM((4, ny), F32),
+            pltpu.VMEM((6, feats), F32),
+            pltpu.VMEM((1, 6), F32),
+            dma((2, zs)),
+            dma((3,)),
+        ],
         name="deliver",
     )(grad_field, sums)
     return grad_probs, grad_weight, grad_bias.reshape(6)

time: 57.7 us -> 57.5 us (level)
    pallas_call x1, Pallas kernels: 2.9 us -> 1.73 us  [per_device(): pl.pallas_call(deliver(feats), out_shape=(jax.ShapeDtypeStruct(probs.shap...]
    pallas_call x1, Pallas kernels: 53.9 us -> 54.9 us  [per_device(): pl.pallas_call(make_kernel(zs, chans, feats, gx, gy, inner, factor), out_...]
where the time goes in v4:
time: 57.5 us; the launch traced here: 57.2 us
  Pallas kernels  56.6 us (98%)
  between operations  0.64 us (1%)
    pallas_call x1, Pallas kernels, per_device(): pl.pallas_call(make_kernel(zs, chans, feats, gx, gy, inner, factor), out_...  54.9 us
    pallas_call x1, Pallas kernels, per_device(): pl.pallas_call(deliver(feats), out_shape=(jax.ShapeDtypeStruct(probs.shap...  1.73 us

profile of v4, /device:TPU:1, one launch (start us, length us, event | category | flops | bytes accessed | tf_op | source)
XLA Modules:
  0.0 57.2 jit_solution(1811334154680055627)
XLA Ops:
  0.6 54.9 %spread_backward.1 = (f32[8,8,8,128]{3,2,1,0:T(8,128)}, f32[4,128]{1,0:T(4,128)}) custom-call(bf16[8,512,128]{2,1,0:T(8,128)(2,1)} %bitcast.2, bf16[6,64]{1,0:T(8,128)(2,1)} %weight_ref.1, f32[6]{0:T(128)} %bias_ref.1, f32[8,8,8,128]{3,2,1,0:T(8,128)} %probs_hbm.1, f32[8,8,8,128]{3,2,1,0:T(8,128)} %cot_hbm.1), custom_call_target="tpu_custom_call" | custom-call | tf_op jit(solution)/shard_map/spread_backward/pallas_call | solution.py:486
  55.5 1.7 %deliver.1 = (f32[8,8,8,128]{3,2,1,0:T(8,128)}, f32[6,64]{1,0:T(8,128)}, f32[1,6]{1,0:T(1,128)}) custom-call(f32[8,8,8,128]{3,2,1,0:T(8,128)} %get-tuple-element.8.field, f32[4,128]{1,0:T(4,128)} %get-tuple-element.9.sums), custom_call_target="tpu_custom_call" | custom-call | tf_op jit(solution)/shard_map/deliver/pallas_call | solution.py:532

commit v5 on v4

--- a/solution.py
+++ b/solution.py
@@ -167,10 +167,6 @@
                 for i, (dx, dy) in enumerate(SIDES)
             ]
 
-        pl.semaphore_wait(barrier, len(greeted))
-        planes, every = pl.ds(0, zs), pl.ds(0, chans)
-        send(row_copies(0, 3, lambda r: probs_hbm.at[planes, every, r], lambda r: hs.at[0, inside, every, r]))
-        send(row_copies(1, 2, lambda r: cot_hbm.at[planes, every, r], lambda r: gs.at[0, inside, every, r]))
         for load in fields_in:
             load.wait()
 
@@ -180,6 +176,10 @@
             sf[0, z, :NX] = of_h + pltpu.roll(of_g, 8, 1)
 
         over_z(pack_fields)
+        pl.semaphore_wait(barrier, len(greeted))
+        planes, every = pl.ds(0, zs), pl.ds(0, chans)
+        send(row_copies(0, 3, lambda r: hs.at[0, inside, every, r], lambda r: hs.at[0, inside, every, r]))
+        send(row_copies(1, 2, lambda r: gs.at[0, inside, every, r], lambda r: gs.at[0, inside, every, r]))
         send(strip_copies(0, sf))
 
         biases = [bias_ref[k] for k in range(6)]
@@ -205,7 +205,7 @@
         send(row_copies(2, 2, k_rows, k_rows))
         send(strip_copies(1, sk))
         outermost = send(
-            far_copies(3, lambda r: cot_hbm.at[planes, every, r], far_g)
+            far_copies(3, lambda r: gs.at[0, inside, every, r], far_g)
             + far_copies(4, k_rows, far_k),
             awaited=False,
         )

time: 57.5 us -> 57.4 us (level)
  no operation moved by 1% of the time
where the time goes in v5:
time: 57.4 us; the launch traced here: 57.1 us
  Pallas kernels  56.5 us (98%)
  between operations  0.64 us (1%)
    pallas_call x1, Pallas kernels, per_device(): pl.pallas_call(make_kernel(zs, chans, feats, gx, gy, inner, factor), out_...  54.7 us
    pallas_call x1, Pallas kernels, per_device(): pl.pallas_call(deliver(feats), out_shape=(jax.ShapeDtypeStruct(probs.shap...  1.73 us

profile of v5, /device:TPU:1, one launch (start us, length us, event | category | flops | bytes accessed | tf_op | source)
XLA Modules:
  0.0 57.1 jit_solution(14253352202115751663)
XLA Ops:
  0.6 54.7 %spread_backward.1 = (f32[8,8,8,128]{3,2,1,0:T(8,128)}, f32[4,128]{1,0:T(4,128)}) custom-call(bf16[8,512,128]{2,1,0:T(8,128)(2,1)} %bitcast.2, bf16[6,64]{1,0:T(8,128)(2,1)} %weight_ref.1, f32[6]{0:T(128)} %bias_ref.1, f32[8,8,8,128]{3,2,1,0:T(8,128)} %probs_hbm.1, f32[8,8,8,128]{3,2,1,0:T(8,128)} %cot_hbm.1), custom_call_target="tpu_custom_call" | custom-call | tf_op jit(solution)/shard_map/spread_backward/pallas_call | solution.py:486
  55.4 1.7 %deliver.1 = (f32[8,8,8,128]{3,2,1,0:T(8,128)}, f32[6,64]{1,0:T(8,128)}, f32[1,6]{1,0:T(1,128)}) custom-call(f32[8,8,8,128]{3,2,1,0:T(8,128)} %get-tuple-element.8.field, f32[4,128]{1,0:T(4,128)} %get-tuple-element.9.sums), custom_call_target="tpu_custom_call" | custom-call | tf_op jit(solution)/shard_map/deliver/pallas_call | solution.py:532

commit v6 on v3

--- a/solution.py
+++ b/solution.py
@@ -434,23 +434,32 @@
 
 
 def deliver(feats):
-    def kernel(field, sums, grad_probs, grad_weight, grad_bias, held, sems):
+    def kernel(field, sums, grad_probs, grad_weight, grad_bias, held, sums_in, weight_out, bias_out, sems, small):
         planes = range(field.shape[0])
         loads = [pltpu.make_async_copy(field.at[z], held.at[z], sems.at[0, z]) for z in planes]
         stores = [pltpu.make_async_copy(held.at[z], grad_probs.at[z], sems.at[1, z]) for z in planes]
+        first = pltpu.make_async_copy(sums, sums_in, small.at[0])
+        last = [
+            pltpu.make_async_copy(weight_out, grad_weight, small.at[1]),
+            pltpu.make_async_copy(bias_out, grad_bias, small.at[2]),
+        ]
+        first.start()
         for load in loads:
             load.start()
+        first.wait()
         for k in range(6):
-            row = sums[k // 2 : k // 2 + 1, :]
+            row = sums_in[k // 2 : k // 2 + 1, :]
             if k % 2:
                 row = pltpu.roll(row, feats, 1)
-            grad_weight[k : k + 1, :] = row[:, :feats]
-        grad_bias[...] = sums[3:4, :6]
+            weight_out[k : k + 1, :] = row[:, :feats]
+        bias_out[...] = sums_in[3:4, :6]
+        for copy in last:
+            copy.start()
         for load, store in zip(loads, stores):
             load.wait()
             store.start()
-        for store in stores:
-            store.wait()
+        for copy in stores + last:
+            copy.wait()
 
     return kernel
 
@@ -524,9 +533,16 @@
             jax.ShapeDtypeStruct((6, feats), F32),
             jax.ShapeDtypeStruct((1, 6), F32),
         ),
-        in_specs=[hbm, vmem],
-        out_specs=(hbm, vmem, vmem),
-        scratch_shapes=[pltpu.VMEM(probs.shape, F32), dma((2, zs))],
+        in_specs=[hbm, hbm],
+        out_specs=(hbm, hbm, hbm),
+        scratch_shapes=[
+            pltpu.VMEM(probs.shape, F32),
+            pltpu.VMEM((4, ny), F32),
+            pltpu.VMEM((6, feats), F32),
+            pltpu.VMEM((1, 6), F32),
+            dma((2, zs)),
+            dma((3,)),
+        ],
         name="deliver",
     )(grad_field, sums)
     return grad_probs, grad_weight, grad_bias.reshape(6)

time: 57.7 us -> 56.5 us (0.979)
  Pallas kernels: 56.8 us -> 55.6 us
    pallas_call x1, Pallas kernels: 2.9 us -> 1.73 us  [per_device(): pl.pallas_call(deliver(feats), out_shape=(jax.ShapeDtypeStruct(probs.shap...]
where the time goes in v6:
time: 56.5 us; the launch traced here: 56.2 us
  Pallas kernels  55.6 us (98%)
  between operations  0.64 us (1%)
    pallas_call x1, Pallas kernels, per_device(): pl.pallas_call(make_kernel(zs, chans, feats, gx, gy, inner, factor), out_...  53.9 us
    pallas_call x1, Pallas kernels, per_device(): pl.pallas_call(deliver(feats), out_shape=(jax.ShapeDtypeStruct(probs.shap...  1.73 us

profile of v6, /device:TPU:1, one launch (start us, length us, event | category | flops | bytes accessed | tf_op | source)
XLA Modules:
  0.0 56.2 jit_solution(14559554354492767005)
XLA Ops:
  0.6 53.9 %spread_backward.1 = (f32[8,8,8,128]{3,2,1,0:T(8,128)}, f32[4,128]{1,0:T(4,128)}) custom-call(bf16[8,512,128]{2,1,0:T(8,128)(2,1)} %bitcast.2, bf16[6,64]{1,0:T(8,128)(2,1)} %weight_ref.1, f32[6]{0:T(128)} %bias_ref.1, f32[8,8,8,128]{3,2,1,0:T(8,128)} %probs_hbm.1, f32[8,8,8,128]{3,2,1,0:T(8,128)} %cot_hbm.1), custom_call_target="tpu_custom_call" | custom-call | tf_op jit(solution)/shard_map/spread_backward/pallas_call | solution.py:483
  54.5 1.7 %deliver.1 = (f32[8,8,8,128]{3,2,1,0:T(8,128)}, f32[6,64]{1,0:T(8,128)}, f32[1,6]{1,0:T(1,128)}) custom-call(f32[8,8,8,128]{3,2,1,0:T(8,128)} %get-tuple-element.8.field, f32[4,128]{1,0:T(4,128)} %get-tuple-element.9.sums), custom_call_target="tpu_custom_call" | custom-call | tf_op jit(solution)/shard_map/deliver/pallas_call | solution.py:529

commit v7 on v6

--- a/solution.py
+++ b/solution.py
@@ -396,7 +396,7 @@
                 value = value + buffer[i]
             return value
 
-        first = exchange(sum_a, me_y, partners_a, sa_sem, ra_sem, payload)
+        first = exchange(sum_b, me_in, partners_b, sb_sem, rb_sem, payload)
 
         for copy in outermost:
             copy.wait_recv()
@@ -421,9 +421,9 @@
         store = pltpu.make_async_copy(g_out, out_hbm, local_sem.at[2 + zs])
         store.start()
 
-        value = gather(sum_a, first, gy)
-        second = exchange(sum_b, me_in, partners_b, sb_sem, rb_sem, value)
-        value = gather(sum_b, second, inner)
+        value = gather(sum_b, first, inner)
+        second = exchange(sum_a, me_y, partners_a, sa_sem, ra_sem, value)
+        value = gather(sum_a, second, gy)
         third = exchange(sum_c, me_out, partners_c, sc_sem, rc_sem, value)
         sum_ref[...] = gather(sum_c, third, outer) * factor
         for copy in pending:

time: 56.5 us -> 57.4 us (1.016)
  Pallas kernels: 55.6 us -> 56.5 us
    pallas_call x1, Pallas kernels: 53.9 us -> 54.7 us  [per_device(): pl.pallas_call(make_kernel(zs, chans, feats, gx, gy, inner, factor), out_...]
where the time goes in v7:
time: 57.4 us; the launch traced here: 57.1 us
  Pallas kernels  56.5 us (98%)
  between operations  0.64 us (1%)
    pallas_call x1, Pallas kernels, per_device(): pl.pallas_call(make_kernel(zs, chans, feats, gx, gy, inner, factor), out_...  54.7 us
    pallas_call x1, Pallas kernels, per_device(): pl.pallas_call(deliver(feats), out_shape=(jax.ShapeDtypeStruct(probs.shap...  1.73 us

profile of v7, /device:TPU:1, one launch (start us, length us, event | category | flops | bytes accessed | tf_op | source)
XLA Modules:
  0.0 57.1 jit_solution(2856416697289913926)
XLA Ops:
  0.6 54.7 %spread_backward.1 = (f32[8,8,8,128]{3,2,1,0:T(8,128)}, f32[4,128]{1,0:T(4,128)}) custom-call(bf16[8,512,128]{2,1,0:T(8,128)(2,1)} %bitcast.2, bf16[6,64]{1,0:T(8,128)(2,1)} %weight_ref.1, f32[6]{0:T(128)} %bias_ref.1, f32[8,8,8,128]{3,2,1,0:T(8,128)} %probs_hbm.1, f32[8,8,8,128]{3,2,1,0:T(8,128)} %cot_hbm.1), custom_call_target="tpu_custom_call" | custom-call | tf_op jit(solution)/shard_map/spread_backward/pallas_call | solution.py:483
  55.4 1.7 %deliver.1 = (f32[8,8,8,128]{3,2,1,0:T(8,128)}, f32[6,64]{1,0:T(8,128)}, f32[1,6]{1,0:T(1,128)}) custom-call(f32[8,8,8,128]{3,2,1,0:T(8,128)} %get-tuple-element.8.field, f32[4,128]{1,0:T(4,128)} %get-tuple-element.9.sums), custom_call_target="tpu_custom_call" | custom-call | tf_op jit(solution)/shard_map/deliver/pallas_call | solution.py:529
